TPU v7x, 256 devices: a whole 4x4x8 slice. The times are simulated.
256 devices in a mesh: group: 2 (over y_hi), wide: 128 (over y_lo, z, x, core).
Axes of the slice: x: 4, y: 4 (y_hi: 2, y_lo: 2; y = y_hi * 2 + y_lo), z: 8, core: 2. Of those that a mesh axis runs over, the one named last changes fastest.
Arguments:
- tokens: bfloat16 [16384, 2880], P('wide'), may hold values from -6 to 6
- routes: int32 [16384, 4], P('wide'), may hold values from 0 to 127, all different within a row; in each aligned block of 128 rows (0 to 127, 128 to 255, ...) at most 8 rows name the same one
- router: bfloat16 [2880, 128], replicated, may hold values from -0.109375 to 0.109375
- gate_codes: int32 [128, 960, 1536], P('wide', None, 'group'), may hold values from 0 to 4095
- gate_scales: int32 [128, 90, 1536], P('wide', None, 'group'), may hold values from -9 to -6
- up_codes: int32 [128, 960, 1536], P('wide', None, 'group'), may hold values from 0 to 4095
- up_scales: int32 [128, 90, 1536], P('wide', None, 'group'), may hold values from -9 to -6
- down_codes: int32 [128, 512, 2880], P('wide', 'group'), may hold values from 0 to 4095
- down_scales: int32 [128, 48, 2880], P('wide', 'group'), may hold values from -8 to -5
- norm_gain: float32 [2880], replicated, may hold values from 0.25 to 1.75
- drafter_weight: bfloat16 [1536, 2880], P(('group', 'wide')), may hold values from -0.109375 to 0.109375
Outputs:
- draft_error: bfloat16 [16384, 1536], P('wide', 'group')
- draft_grad: bfloat16 [1536, 2880], P(('group', 'wide'))
Inputs may be any that keep to these rules, and one draw needn't show every extreme that they name: `routes`: each token names 4 different experts; among the 128 tokens of one device no expert is named more than 8 times.
All inputs are finite; a program needn't handle non-finite values.
Results may differ from a plain program's by a relative error of at most 0.007.
Values may be sent and summed in bfloat16 or wider, within the bound.
A program may use at most 192 MiB of HBM per device.

v0:
```python
import math

import jax
import jax.numpy as jnp
from jax import lax
from jax.sharding import PartitionSpec as P


def passed_along(value, axis, steps):
    count = lax.axis_size(axis)
    first, last = (max(0, -steps), min(count, count - steps))
    return lax.ppermute(value, axis, [(source, source + steps) for source in range(first, last)])


def dequantize(packed, exponents):
    shifts = 4 * jnp.arange(3, dtype=jnp.int32)
    nibble = packed[:, None, :] >> shifts[None, :, None] & 15
    magnitude = nibble & 7
    level = magnitude.astype(jnp.bfloat16)
    values = jnp.where(magnitude < 4, level * 0.5, jnp.where(magnitude == 7, 6.0, level - 2.0))
    values = jnp.where(nibble >= 8, -values, values)
    row_count = packed.shape[0] * 3
    values = values.reshape(row_count, packed.shape[1])
    multiplier = jnp.repeat(
        jnp.exp2(exponents.astype(jnp.float32)).astype(jnp.bfloat16), 32, axis=0
    )
    return values * multiplier


def shards(
    tokens,
    routes,
    router,
    gate_codes,
    gate_scales,
    up_codes,
    up_scales,
    down_codes,
    down_scales,
    norm_gain,
    drafter_weight,
):
    tok_rows, model_width = tokens.shape
    top_count = routes.shape[1]
    expert_count = router.shape[1]
    wide_count = lax.axis_size("wide")
    slot_count = 2 * tok_rows * top_count // expert_count
    route_rows = tok_rows * top_count
    logits = jnp.dot(tokens, router, preferred_element_type=jnp.float32)
    route_weight = jax.nn.sigmoid(jnp.take_along_axis(logits, routes, axis=1)).reshape(-1)
    flat_routes = routes.reshape(-1)
    onehot = (flat_routes[:, None] == jnp.arange(expert_count, dtype=jnp.int32)[None, :]).astype(
        jnp.int32
    )
    running = jnp.cumsum(onehot, axis=0)
    slot_index = jnp.sum(onehot * (running - 1), axis=1)
    dest_index = flat_routes * slot_count + slot_index
    source_of = (
        jnp.zeros((expert_count * slot_count,), jnp.int32)
        .at[dest_index]
        .set(jnp.arange(route_rows, dtype=jnp.int32))
    )
    filled = (
        jnp.zeros((expert_count * slot_count,), jnp.bfloat16)
        .at[dest_index]
        .set(jnp.ones((route_rows,), jnp.bfloat16))
    )
    buffer = (tokens[source_of // top_count] * filled[:, None]).reshape(
        expert_count, slot_count, model_width
    )
    gate_w = dequantize(gate_codes[0], gate_scales[0])
    up_w = dequantize(up_codes[0], up_scales[0])
    down_w = dequantize(down_codes[0], down_scales[0])
    arrived = lax.all_to_all(buffer, "wide", split_axis=0, concat_axis=0, tiled=True)
    frame = arrived.shape
    inputs = arrived.reshape(-1, model_width)
    gate_act = jnp.dot(inputs, gate_w, preferred_element_type=jnp.float32)
    up_act = jnp.dot(inputs, up_w, preferred_element_type=jnp.float32)
    hidden = (jax.nn.silu(gate_act) * up_act).astype(jnp.bfloat16)
    outputs = jnp.dot(hidden, down_w, preferred_element_type=jnp.float32).reshape(frame)
    summed = lax.psum_scatter(outputs, "group", scatter_dimension=2, tiled=True).astype(
        jnp.bfloat16
    )
    returned = lax.all_to_all(summed, "wide", split_axis=0, concat_axis=0, tiled=True)
    share_width = returned.shape[2]
    gathered = returned.reshape(expert_count * slot_count, share_width)[dest_index]
    weighted = gathered.astype(jnp.float32) * route_weight[:, None]
    share = jnp.sum(weighted.reshape(tok_rows, top_count, share_width), axis=1).astype(jnp.bfloat16)
    feature_b = lax.all_gather(share, "group", axis=1, tiled=True).astype(jnp.float32)
    mean_square = jnp.sum(feature_b * feature_b, axis=1, keepdims=True) / model_width
    normed = (feature_b * lax.rsqrt(mean_square + 1e-05) * norm_gain[None, :]).astype(jnp.bfloat16)
    predicted = lax.dot_general(
        normed,
        lax.all_gather(drafter_weight, "wide", axis=0, tiled=True),
        (((1,), (1,)), ((), ())),
        preferred_element_type=jnp.float32,
    )
    out_share = predicted.shape[1]
    own_target = lax.dynamic_slice_in_dim(normed, lax.axis_index("group") * out_share, out_share, 1)
    following = passed_along(own_target[:1], "wide", -1)
    target = jnp.concatenate([own_target[1:], following], axis=0)
    position = lax.axis_index("wide") * tok_rows + jnp.arange(tok_rows, dtype=jnp.int32)
    inside = position < tok_rows * wide_count - 1
    draft_error = jnp.where(inside[:, None], predicted - target.astype(jnp.float32), 0.0).astype(
        jnp.bfloat16
    )
    grad_scale = 1.0 / math.sqrt(tok_rows * wide_count)
    draft_grad = lax.psum_scatter(
        lax.dot_general(
            draft_error, normed, (((0,), (0,)), ((), ())), preferred_element_type=jnp.float32
        )
        * grad_scale,
        "wide",
        scatter_dimension=0,
        tiled=True,
    )
    return (draft_error, draft_grad.astype(jnp.bfloat16))


def solution(mesh):
    placed = (
        P("wide", None),
        P("wide", None),
        P(),
        P("wide", None, "group"),
        P("wide", None, "group"),
        P("wide", None, "group"),
        P("wide", None, "group"),
        P("wide", "group", None),
        P("wide", "group", None),
        P(),
        P(("group", "wide"), None),
    )
    return jax.shard_map(
        shards,
        mesh=mesh,
        in_specs=placed,
        out_specs=(P("wide", "group"), P(("group", "wide"), None)),
        check_vma=False,
    )
```

profile of v0, /device:TPU:16, one launch (start us, length us, event | category | flops | bytes accessed | tf_op | source)
XLA Modules:
  0.0 1214.9 jit_solution(14038733838799831804)
XLA Ops:
  8.0 0.8 broadcast_multiply_fusion
  8.8 0.8 copy.66
  9.8 1.5 copy.70
  11.9 0.2 fusion.23
  12.2 2.4 scatter_custom_fusion
  14.7 3.8 scatter_custom_fusion.1
  18.5 6.6 gather_fusion
  25.1 5.9 bitcast_multiply_fusion
  31.0 14.3 %all-to-all-start = ((bf16[128,8,2880]{2,1,0:T(8,128)(2,1)}), bf16[128,8,2880]{2,1,0:T(8,128)(2,1)}, u32[]{:S(2)}, u32[]{:S(2)}) async-start(bf16[128,8,2880]{2,1,0:T(8,128)(2,1)} %bitcast_multiply_fusion), calls=%async_computation | async-start | bytes 12058624 | tf_op jit(solution)/shard_map/all_to_all | solution.py:74
  45.6 3.5 copy.71
  49.1 8.0 shift_right_arithmetic.99
  57.1 13.6 %shift_right_arithmetic.100 = s32[24,32,2880]{2,1,0:T(8,128)} reshape(s32[256,3,2880]{2,1,0:T(4,128)} %shift_right_arithmetic.99) | data formatting | bytes 17694720 | tf_op jit(solution)/shard_map/shift_right_arithmetic | solution.py:17
  70.9 7.4 shift_right_arithmetic.88
  78.3 14.3 %shift_right_arithmetic.89 = s32[90,32,768]{2,1,0:T(8,128)} reshape(s32[960,3,768]{2,1,0:T(4,128)} %shift_right_arithmetic.88) | data formatting | bytes 17694720 | tf_op jit(solution)/shard_map/shift_right_arithmetic | solution.py:17
  92.7 0.4 shift_right_arithmetic.91
  93.0 7.4 shift_right_arithmetic.95
  100.5 14.4 %shift_right_arithmetic.96 = s32[90,32,768]{2,1,0:T(8,128)} reshape(s32[960,3,768]{2,1,0:T(4,128)} %shift_right_arithmetic.95) | data formatting | bytes 17694720 | tf_op jit(solution)/shard_map/shift_right_arithmetic | solution.py:17
  114.9 0.4 exponential_convert_fusion.1
  115.3 0.4 exponential_convert_fusion.2
  115.8 9.6 fusion.10
  125.4 13.0 %fusion.11 = (bf16[90,32,768]{2,1,0:T(8,128)(2,1)}, bf16[90,32,768]{2,1,0:T(8,128)(2,1)}) fusion(s32[90,32,768]{2,1,0:T(8,128)} %shift_right_arithmetic.89, s32[90,32]{1,0:T(8,128)S(1)} %shift_right_arithmetic.91, bf16[90,768]{1,0:T(8,128)(2,1)S(1)} %get-tuple-element.5, bf16[90,768]{1,0:T(8,128)(2,1)S(1)} %get-tuple-element.4, s32[90,32,768]{2,1,0:T(8,128)S(1)} %copy-done.1), kind=kLoop, calls=%fused_computation.30 | loop fusion | flops 101744640 | bytes 26830080 | tf_op jit(solution)/shard_map/mul | solution.py:27
  138.3 42.0 %all-to-all-done = bf16[128,8,2880]{2,1,0:T(8,128)(2,1)} async-done(((bf16[128,8,2880]{2,1,0:T(8,128)(2,1)}), bf16[128,8,2880]{2,1,0:T(8,128)(2,1)}, u32[]{:S(2)}, u32[]{:S(2)}) %all-to-all-start) | async-done | bytes 5898272 | tf_op jit(solution)/shard_map/all_to_all | solution.py:74
  180.4 8.5 fusion.3
  188.9 7.6 fusion.20
  196.6 7.7 fusion.15
  204.3 0.5 all-gather.3.cloned.1.call-update
  204.8 136.5 %reduce-scatter.2.cloned.1.call-done = f32[128,8,1440]{0,2,1:T(8,128)} async-done(((f32[128,8,2880]{0,2,1:T(8,128)}), f32[128,8,1440]{0,2,1:T(8,128)}) %reduce-scatter.2.cloned.1.call-update) | async-done | bytes 5898256 | tf_op jit(solution)/shard_map/reduce_scatter | solution.py:81
  341.3 4.7 convert_element_type.118
  346.0 5.0 copy.74
  351.1 16.5 %all-to-all-start.1 = ((bf16[128,8,1440]{2,1,0:T(8,128)(2,1)}), bf16[128,8,1440]{2,1,0:T(8,128)(2,1)}, u32[]{:S(2)}, u32[]{:S(2)}) async-start(bf16[128,8,1440]{2,1,0:T(8,128)(2,1)} %copy.74), calls=%async_computation.2 | async-start | bytes 6291456 | tf_op jit(solution)/shard_map/all_to_all | solution.py:84
  367.9 0.4 fusion.35
  368.3 3.6 gather_fusion.2
  372.2 78.3 %all-to-all-done.1 = bf16[128,8,1440]{2,1,0:T(8,128)(2,1)} async-done(((bf16[128,8,1440]{2,1,0:T(8,128)(2,1)}), bf16[128,8,1440]{2,1,0:T(8,128)(2,1)}, u32[]{:S(2)}, u32[]{:S(2)}) %all-to-all-start.1) | async-done | bytes 2949152 | tf_op jit(solution)/shard_map/all_to_all | solution.py:84
  450.5 5.9 gather_fusion.1
  456.4 2.2 reshape.269
  458.6 4.2 multiply_reduce_fusion
  463.0 10.9 all_gather.6
  473.9 0.3 copy.79
  474.3 0.2 fusion.17
  474.5 0.2 fusion.19
  474.9 1.3 collective-permute-start
  476.2 0.6 dynamic-slice
  477.4 71.4 %all-gather.3.cloned.1.call-done = bf16[128,6,2880]{2,1,0:T(8,128)(2,1)} async-done(((bf16[1,6,2880]{2,1,0:T(8,128)(2,1)}), bf16[128,6,2880]{2,1,0:T(8,128)(2,1)}) %all-gather.3.cloned.1.call-update) | async-done | bytes 4423696 | tf_op jit(solution)/shard_map/all_gather | solution.py:94
  548.8 8.2 reshape.315
  557.2 3.7 select_convert_fusion
  560.9 4.9 convolution_multiply_fusion
  565.7 639.8 %all-reduce.2 = bf16[768,2880]{1,0:T(8,128)(2,1)} all-reduce(f32[768,2880]{1,0:T(8,128)} %convolution_multiply_fusion), channel_id=3, replica_groups=mesh['group'=2,'wide'=128] {'wide'}, use_global_device_ids=true, to_apply=%region_8.9.clone | all-reduce | flops 2211840 | bytes 13271040
  1205.5 1.5 dynamic-slice_convert_fusion
  (66 shorter events, 2.6 us)
Async XLA Ops:
  8.0 359.8 %copy-start = (bf16[2880,128]{1,0:T(8,128)(2,1)S(1)}, bf16[2880,128]{1,0:T(8,128)(2,1)}, u32[]{:S(2)}) copy-start(bf16[2880,128]{1,0:T(8,128)(2,1)} %param.13) | copy-start | bytes 2211844
  31.0 149.4 %all-to-all-start = ((bf16[128,8,2880]{2,1,0:T(8,128)(2,1)}), bf16[128,8,2880]{2,1,0:T(8,128)(2,1)}, u32[]{:S(2)}, u32[]{:S(2)}) async-start(bf16[128,8,2880]{2,1,0:T(8,128)(2,1)} %bitcast_multiply_fusion), calls=%async_computation | async-start | bytes 12058624 | tf_op jit(solution)/shard_map/all_to_all | solution.py:74
  45.3 296.0 %reduce-scatter.2.cloned.1.call-start = ((), (), s32[]{:S(2)}) async-start(), calls=%async_computation.3 | async-start | bytes 17694720 | tf_op jit(solution)/shard_map/reduce_scatter | solution.py:81
  100.4 14.4 %copy-start.6 = (s32[1,90,768]{2,0,1:T(1,128)S(1)}, s32[1,90,768]{2,0,1:T(1,128)}, u32[]{:S(2)}) copy-start(s32[1,90,768]{2,0,1:T(1,128)} %param.17) | copy-start | bytes 829444
  100.5 14.8 %copy-start.7 = (s32[1,90,768]{2,0,1:T(1,128)S(1)}, s32[1,90,768]{2,0,1:T(1,128)}, u32[]{:S(2)}) copy-start(s32[1,90,768]{2,0,1:T(1,128)} %param.15) | copy-start | bytes 829444
  100.5 15.2 %copy-start.5 = (s32[1,24,2880]{2,1,0:T(8,128)S(1)}, s32[1,24,2880]{2,1,0:T(8,128)}, u32[]{:S(2)}) copy-start(s32[1,24,2880]{2,1,0:T(8,128)} %param.19) | copy-start | bytes 829444
  115.8 9.6 copy-start.1
  180.4 8.5 copy-start.2
  180.4 16.2 %slice-start = ((s8[4521984]{0:T(1024)(128)(4,1)}), s8[4194304]{0:T(1024)(128)(4,1)S(1)}, s32[]{:S(2)}) async-start(s8[4521984]{0:T(1024)(128)(4,1)} %bitcast.53), calls=%async_computation.5 | async-start | bytes 8388608
  188.9 7.6 slice-start.1
  204.3 344.5 %all-gather.3.cloned.1.call-start = ((), (), s32[]{:S(2)}) async-start(), calls=%async_computation.4 | async-start | bytes 6076416 | tf_op jit(solution)/shard_map/all_gather | solution.py:94
  351.0 16.5 %copy-start.8 = (s32[128,4]{0,1:T(4,128)S(1)}, s32[128,4]{0,1:T(4,128)}, u32[]{:S(2)}) copy-start(s32[128,4]{0,1:T(4,128)} %param.12) | copy-start | bytes 6148
  351.1 16.8 %copy-start.3 = (bf16[128,2880]{0,1:T(8,128)(2,1)S(1)}, bf16[128,2880]{0,1:T(8,128)(2,1)}, u32[]{:S(2)}) copy-start(bf16[128,2880]{0,1:T(8,128)(2,1)} %param.11) | copy-start | bytes 2211844
  351.1 99.5 %all-to-all-start.1 = ((bf16[128,8,1440]{2,1,0:T(8,128)(2,1)}), bf16[128,8,1440]{2,1,0:T(8,128)(2,1)}, u32[]{:S(2)}, u32[]{:S(2)}) async-start(bf16[128,8,1440]{2,1,0:T(8,128)(2,1)} %copy.74), calls=%async_computation.2 | async-start | bytes 6291456 | tf_op jit(solution)/shard_map/all_to_all | solution.py:84
  458.6 15.9 %copy-start.9 = (f32[2880]{0:T(1024)S(1)}, f32[2880]{0:T(1024)}, u32[]{:S(2)}) copy-start(f32[2880]{0:T(1024)} %param.20) | copy-start | bytes 34564
  458.6 17.6 %copy-start.10 = (u32[256]{0:T(256)S(1)}, u32[256]{0:T(256)}, u32[]{:S(2)}) copy-start(u32[256]{0:T(256)} %constant.127) | copy-start | bytes 3076
  474.9 82.3 %collective-permute-start = (bf16[1,768]{1,0:T(2,128)(2,1)S(1)}, bf16[1,768]{1,0:T(2,128)(2,1)S(1)}, u32[]{:S(2)}, u32[]{:S(2)}) collective-permute-start(bf16[1,768]{1,0:T(2,128)(2,1)S(1)} %constant_dynamic-slice_fusion), channel_id=1, source_target_pairs={{1,0},{2,1},{3,2},{4,3},{5,4},{6,5},{7,6},{8,7},{9,8},{10,9},{11,1... | collective-permute-start | bytes 4616 | tf_op jit(solution)/shard_map/ppermute | solution.py:12
  560.9 4.9 copy-start.4
Sparse Core Ops, SparseCore 0:
  204.4 136.9 reduce-scatter.1
Sparse Core Ops, SparseCore 1:
  206.6 342.1 all-gather.2
where the time goes:
time: 1220 us; the launch traced here: 1210 us
  blocking collectives  651 us (53%)
  waiting for transfers between devices  329 us (27%)
  local copies, waits for them, and re-layouts  113 us (9%)
  other arithmetic  39.9 us (3%)
  matrix products  32.7 us (3%)
  starting transfers between devices  32.4 us (3%)
  between operations  17 us (1%)
    unnamed x1, blocking collectives  640 us
    reduce_scatter x1, waiting for transfers between devices, shards(): lax.psum_scatter(outputs, 'group', scatter_dimension=2, tiled=True)  136 us
    all_to_all x1, waiting for transfers between devices, shards(): lax.all_to_all(summed, 'wide', split_axis=0, concat_axis=0, tiled=True)  78.3 us
    all_gather x1, waiting for transfers between devices, shards(): lax.all_gather(drafter_weight, 'wide', axis=0, tiled=True)  71.4 us
    shift_right_arithmetic x11, local copies, waits for them, and re-layouts, dequantize(): nibble = packed[:, None, :] >> shifts[None, :, None] & 15  69.3 us
    all_to_all x1, waiting for transfers between devices, shards(): lax.all_to_all(buffer, 'wide', split_axis=0, concat_axis=0, tiled=True)  42 us
  transfers between devices with their start and end apart: 5, of which 4 were waited for; matrix products, arithmetic and copies ran while one was open for 11% of the time, Pallas kernels for 0%

commit v1 on v0

v1 whole, which is shorter than its diff:
```python
import functools
import math

import jax
import jax.numpy as jnp
from jax import lax
from jax.experimental import pallas as pl
from jax.experimental.pallas import tpu as pltpu
from jax.sharding import PartitionSpec as P

MESH = pl.DeviceIdType.MESH
F32 = jnp.float32
BF16 = jnp.bfloat16

D = 2880
TOK = 128
NZ = 8
PLANE = 16
SLOT = 8
SLABS = TOK // SLOT
UNITS = 768
WORDS = 960
BLOCKS = SLABS + 1
META = 6


def place():
    group, wide = lax.axis_index("group"), lax.axis_index("wide")
    y, z, x, c = wide // 64, (wide // 8) % 8, (wide // 2) % 4, wide % 2
    return group, wide, y, z, x, c


def wide_of(y, z, x, c):
    return y * 64 + z * 8 + x * 2 + c


def plane_wide(p, z):
    return (p // 8) * 64 + z * 8 + p % 8


def iota(shape, dim, kind=jnp.int32):
    return lax.broadcasted_iota(jnp.int32, shape, dim).astype(kind)


def dot(a, b):
    return jnp.dot(a, b, preferred_element_type=F32)


def remote(src, dst, send, recv, device):
    return pltpu.make_async_remote_copy(
        src_ref=src, dst_ref=dst, send_sem=send, recv_sem=recv, device_id=device, device_id_type=MESH
    )


def spread(tokens):
    parts = []
    for start, length in [(384 * b, 384) for b in range(7)] + [(2688, 192)]:
        third = length // 3
        row = iota((length, length), 0)
        column = iota((length, length), 1)
        order = (row == 3 * (column % third) + column // third).astype(F32).astype(BF16)
        parts.append(dot(tokens[:, start : start + length], order).astype(BF16))
    return parts


def prep_kernel(tokens_ref, routes_ref, router_ref, weight_ref, out_ref):
    tokens = tokens_ref[...]
    logits = dot(tokens, router_ref[...])
    weight = jax.nn.sigmoid(logits).T
    column = 0
    for part in spread(tokens):
        width = part.shape[1]
        out_ref[0:SLABS, :, column : column + width] = part.astype(F32).reshape(SLABS, SLOT, width).astype(BF16)
        column += width
    out_ref[SLABS, :, :] = weight_ref[...]
    experts = iota((TOK, TOK), 0)
    routes, high, low = [], [], []
    for k in range(4):
        route = routes_ref[k : k + 1, :]
        chosen = jnp.sum(jnp.where(experts == route, weight, 0.0), axis=0, keepdims=True)
        top = chosen.astype(BF16).astype(F32)
        routes.append(route.astype(F32))
        high.append(top)
        low.append(chosen - top)
    line = jnp.concatenate(routes + high + low, axis=1)
    slab = weight_ref[:, 0 : 12 * TOK].astype(F32)
    row = iota((SLOT, 12 * TOK), 0)
    out_ref[SLABS, :, 0 : 12 * TOK] = jnp.where(row == META, line, slab).astype(BF16)


def level(nibble):
    m = nibble & 7
    twice = m + jnp.maximum(m - 4, 0) + 2 * jnp.maximum(m - 6, 0)
    return twice.astype(F32)


def unpack(words, j, scales):
    nibble = (words >> (4 * j)) & 15
    half = jnp.exp2((scales - 1).astype(F32))
    return level(nibble) * jnp.where(nibble >= 8, -half, half)


def scale_rows(ref, q, j, width):
    r = iota((32, width), 0)
    block = (3 * r + j) // 32
    rows = [ref[pl.ds(3 * q + n, 1), :] for n in range(3)]
    return jnp.where(block == 0, rows[0], jnp.where(block == 1, rows[1], rows[2]))


def dequant_in(codes, scales, out, q, base, third):
    words = codes[pl.ds(pl.multiple_of(32 * q, 32), 32), :]
    for j in range(3):
        values = unpack(words, j, scale_rows(scales, q, j, words.shape[1]))
        out[pl.ds(pl.multiple_of(base + third * j, 32), 32), :] = values.astype(BF16)


def dequant_wide(codes, scales, out, first, last):
    def step(q, carry):
        dequant_in(codes, scales, out, q, (q // 4) * 384 + (q % 4) * 32, 128)
        return carry

    lax.fori_loop(first, min(last, 28), step, 0)
    for q in range(28, last):
        dequant_in(codes, scales, out, q, 2688 + (q - 28) * 32, 64)


def dispatch_kernel(
    blk, gc, gs, uc, us, dc, ds, xr, wg, wu, wd, comb, wz,
    agb, snd, gcv, gsv, ucv, usv, dcv, dsv, code_sem, zsend, zrecv, psend, precv, loc,
):
    group, wide, y, z, x, c = place()
    p_me = y * 8 + x * 2 + c
    right = (group, wide_of(y, (z + 1) % 8, x, c))
    left = (group, wide_of(y, (z + 7) % 8, x, c))

    barrier = pltpu.get_barrier_semaphore()
    for neighbour in (left, right):
        pl.semaphore_signal(barrier, inc=1, device_id=neighbour, device_id_type=MESH)

    def greet(j, carry):
        p = (p_me + j) % PLANE
        pl.semaphore_signal(barrier, inc=1, device_id=(group, plane_wide(p, z)), device_id_type=MESH)
        return carry

    lax.fori_loop(1, PLANE, greet, 0)

    def greet_other(j, carry):
        p = (1 - y) * 8 + j
        pl.semaphore_signal(barrier, inc=1, device_id=(1 - group, plane_wide(p, z)), device_id_type=MESH)
        return carry

    lax.fori_loop(0, 8, greet_other, 0)

    code_copies = [
        pltpu.make_async_copy(a, b, code_sem.at[n])
        for n, (a, b) in enumerate([(gc, gcv), (gs, gsv), (uc, ucv), (us, usv), (dc, dcv), (ds, dsv)])
    ]
    for copy in code_copies:
        copy.start()
    pl.semaphore_wait(barrier, 25)

    sigma = 1 - 2 * c
    sends = []

    def forward(source, s, device, n):
        copy = remote(source, agb.at[s], zsend.at[n], zrecv.at[n], device)
        copy.start()
        sends.append(copy)

    def arrived(s, n):
        remote(blk, agb.at[s], zsend.at[n], zrecv.at[n], right).wait_recv()

    upper = (iota((TOK, TOK), 0) < iota((TOK, TOK), 1)).astype(F32).astype(BF16)
    p_rows = iota((PLANE, 1), 0)
    experts = ((p_rows // 8) * 64 + z * 8 + p_rows % 8).astype(F32)

    def relay(source, s):
        meta = source[SLABS, :, 0 : 12 * TOK].astype(F32)[META : META + 1, :]
        named = jnp.zeros((PLANE, TOK), F32)
        weight = jnp.zeros((PLANE, TOK), F32)
        for k in range(4):
            hit = (experts == meta[:, k * TOK : (k + 1) * TOK]).astype(F32)
            value = meta[:, (4 + k) * TOK : (5 + k) * TOK] + meta[:, (8 + k) * TOK : (9 + k) * TOK]
            named = named + hit
            weight = weight + hit * value
        rank = dot(named.astype(BF16), upper)
        slot = iota((PLANE, SLOT, TOK), 1, F32)
        pick = jnp.where(rank[:, None, :] == slot, named[:, None, :], 0.0)
        weighted = (pick * weight[:, None, :]).reshape(TOK, TOK).T
        top = weighted.astype(BF16)
        comb[s, 0] = top
        comb[s, 1] = (weighted - top.astype(F32)).astype(BF16)
        rows = dot(pick.reshape(TOK, TOK).astype(BF16), source[0:SLABS].reshape(TOK, D))
        snd[s] = rows.reshape(PLANE, SLOT, D).astype(BF16)
        wz[s] = source[SLABS]
        pltpu.make_async_copy(snd.at[s, p_me], xr.at[s, p_me], loc.at[s]).start()

        def send(j, carry):
            p = (p_me + j) % PLANE
            across = ((p // 8 + y) % 2) * (s % 2)
            remote(
                snd.at[s, p], xr.at[s, p_me], psend.at[s], precv.at[s],
                ((group + across) % 2, plane_wide(p, z)),
            ).start()
            return carry

        lax.fori_loop(1, PLANE, send, 0)

    forward(blk, z, right, 0)
    forward(blk, z, left, 1)
    relay(blk, z)
    code_copies[0].wait()
    code_copies[1].wait()
    dequant_wide(gcv, gsv, wg, 0, 8)
    for k in (1, 2, 3):
        back, ahead = (z + 8 - k) % 8, (z + k) % 8
        arrived(back, 2 * k - 2)
        if k < 3:
            forward(agb.at[back], back, right, 2 * k)
        arrived(ahead, 2 * k - 1)
        if k < 3:
            forward(agb.at[ahead], ahead, left, 2 * k + 1)
        else:
            far = (z + 8 - 3 * sigma) % 8
            forward(agb.at[far], far, (group, wide_of(y, (z + 8 + sigma) % 8, x, c)), 6)
        relay(agb.at[back], back)
        relay(agb.at[ahead], ahead)
        if k == 1:
            dequant_wide(gcv, gsv, wg, 8, 30)
        elif k == 2:
            code_copies[2].wait()
            code_copies[3].wait()
            dequant_wide(ucv, usv, wu, 0, 30)
        else:
            code_copies[4].wait()
            code_copies[5].wait()

            def down_all(q, carry):
                words = dcv[pl.ds(pl.multiple_of(32 * q, 32), 32), :]
                for j in range(3):
                    values = unpack(words, j, scale_rows(dsv, q, j, D))
                    wd[pl.ds(pl.multiple_of(256 * j + 32 * q, 32), 32), :] = values.astype(BF16)
                return carry

            lax.fori_loop(0, 8, down_all, 0)
    opposite = (z + 4) % 8
    arrived(opposite, 6)
    relay(agb.at[opposite], opposite)
    for copy in sends:
        copy.wait_send()
    for s in range(NZ):
        pltpu.make_async_copy(snd.at[0, 0], xr.at[0, 0], loc.at[s]).wait()
        whole = remote(snd.at[s, pl.ds(0, 15)], xr.at[s, pl.ds(0, 15)], psend.at[s], precv.at[s], right)
        whole.wait_send()
        whole.wait_recv()


def expert_kernel(
    xr, wg, wu, wd, comb, wz, gain, normed_ref, wall,
    hid, snd, ret, maj, mnr, shr, xch, loc, wloc, psend, precv, rsend, rrecv, xsem, wsend, wrecv,
):
    group, wide, y, z, x, c = place()
    p_me = y * 8 + x * 2 + c
    other = (1 - group, wide)
    core = (group, wide_of(y, z, x, 1 - c))
    sigma = 1 - 2 * c
    ahead = (group, wide_of(y, (z + 8 + sigma) % 8, x, c))
    behind = (group, wide_of(y, (z + 8 - sigma) % 8, x, c))

    barrier = pltpu.get_barrier_semaphore()
    for neighbour in (ahead, behind, other):
        pl.semaphore_signal(barrier, inc=1, device_id=neighbour, device_id_type=MESH)

    def greet(j, carry):
        p = (p_me + j) % PLANE
        pl.semaphore_signal(barrier, inc=1, device_id=(group, plane_wide(p, z)), device_id_type=MESH)
        return carry

    lax.fori_loop(1, PLANE, greet, 0)

    pl.semaphore_wait(barrier, 18)

    keep = pltpu.make_async_copy(wz, wall.at[c, y, x], wloc)
    keep.start()

    def share_x(j, carry):
        remote(wz, wall.at[c, y, x], wsend.at[0], wrecv.at[0], (group, wide_of(y, z, (x + j) % 4, c))).start()
        return carry

    lax.fori_loop(1, 4, share_x, 0)
    share_y = remote(wall.at[c, y], wall.at[c, y], wsend.at[1], wrecv.at[1], (group, wide_of(1 - y, z, x, c)))
    share_c = remote(wall.at[c], wall.at[c], wsend.at[2], wrecv.at[2], core)

    def hidden(n, carry):
        inputs = xr[pl.ds(2 * n, 2)].reshape(256, D)
        gate = dot(inputs, wg[...])
        up = dot(inputs, wu[...])
        act = (jax.nn.silu(gate) * up).astype(BF16)
        row = iota((UNITS, UNITS), 0)
        column = iota((UNITS, UNITS), 1)
        order = (row == 3 * (column % 256) + column // 256).astype(F32).astype(BF16)
        hid[pl.ds(pl.multiple_of(256 * n, 256), 256), :] = dot(act, order).astype(BF16)
        return carry

    lax.fori_loop(0, 4, hidden, 0)

    def source(d):
        return (z + 8 + d * sigma) % 8

    def down(d):
        s = source(d)
        rows = dot(hid[pl.ds(pl.multiple_of(TOK * s, TOK), TOK), :], wd[...])
        snd[s] = rows.reshape(PLANE, SLOT, D).astype(BF16)
        pltpu.make_async_copy(snd.at[s, p_me], ret.at[s, p_me], loc.at[s]).start()

        def send(j, carry):
            p = (p_me + j) % PLANE
            remote(
                snd.at[s, p], ret.at[s, p_me], psend.at[s], precv.at[s], (group, plane_wide(p, z))
            ).start()
            return carry

        lax.fori_loop(1, PLANE, send, 0)

    def combined(d):
        s = source(d)
        pltpu.make_async_copy(snd.at[s, p_me], ret.at[s, p_me], loc.at[s]).wait()
        remote(
            snd.at[s, pl.ds(0, 15)], ret.at[s, pl.ds(0, 15)], psend.at[s], precv.at[s], core
        ).wait_recv()
        rows = ret[s].reshape(TOK, D)
        return dot(comb[s, 0], rows) + dot(comb[s, 1], rows)

    sends = []

    def hop(buffer, k, device, n):
        copy = remote(buffer.at[k], buffer.at[k - 1], rsend.at[n, k], rrecv.at[n, k - 1], device)
        copy.start()
        sends.append(copy)

    def landed(buffer, k, n):
        remote(buffer.at[k], buffer.at[k], rsend.at[n, k], rrecv.at[n, k], ahead).wait_recv()

    down(4)
    down(3)
    down(-3)
    maj[4] = combined(4).astype(BF16)
    hop(maj, 4, ahead, 0)
    down(2)
    down(-2)
    mnr[3] = combined(-3).astype(BF16)
    hop(mnr, 3, behind, 1)
    part = combined(3)
    landed(maj, 3, 0)
    maj[3] = (maj[3].astype(F32) + part).astype(BF16)
    hop(maj, 3, ahead, 0)
    keep.wait()
    three = remote(
        wall.at[c, y, pl.ds(0, 3)], wall.at[c, y, pl.ds(0, 3)], wsend.at[0], wrecv.at[0], core
    )
    three.wait_recv()
    share_y.start()
    for k in (2, 1):
        if k == 2:
            down(1)
            down(-1)
            down(0)
        part = combined(-k)
        landed(mnr, k, 1)
        mnr[k] = (mnr[k].astype(F32) + part).astype(BF16)
        hop(mnr, k, behind, 1)
        part = combined(k)
        landed(maj, k, 0)
        maj[k] = (maj[k].astype(F32) + part).astype(BF16)
        hop(maj, k, ahead, 0)
    part = combined(0)
    share_y.wait_recv()
    share_c.start()
    landed(mnr, 0, 1)
    part = part + mnr[0].astype(F32)
    landed(maj, 0, 0)
    part = part + maj[0].astype(F32)
    shr[...] = part.astype(BF16)
    swap = remote(shr, xch, xsem.at[0], xsem.at[1], other)
    swap.start()
    swap.wait()
    feature = (shr[...].astype(F32) + xch[...].astype(F32)).astype(BF16).astype(F32)
    mean_square = jnp.sum(feature * feature, axis=1, keepdims=True) / D
    normed_ref[...] = (feature * lax.rsqrt(mean_square + 1e-05) * gain[...]).astype(BF16)
    for copy in sends:
        copy.wait_send()
    for s in range(NZ):
        remote(
            snd.at[s, pl.ds(0, 15)], ret.at[s, pl.ds(0, 15)], psend.at[s], precv.at[s], core
        ).wait_send()
    three.wait_send()
    share_y.wait_send()
    share_c.wait()


def drafter_order(shape, row_dim, padded):
    feature = iota(shape, row_dim)
    q = iota(shape, 1 - row_dim)
    if padded:
        c, y, x, z, i = q // 512, (q // 256) % 2, (q // 64) % 4, (q // 8) % 8, q % 8
        own = y * 384 + z * 48 + x * 12 + c * 6 + i
        return ((feature == own) & (i < 6)).astype(F32).astype(BF16)
    c, z, y, x, i = q // 384, (q // 48) % 8, (q // 24) % 2, (q // 6) % 4, q % 6
    own = y * 384 + z * 48 + x * 12 + c * 6 + i
    return (feature == own).astype(F32).astype(BF16)


def drafter_kernel(
    grad_scale, normed, wall, error_ref, grad_ref,
    nall, first, err, eall, gsum, maj, mnr, slab, fin, fsem, nsem, esem, rsend, rrecv, psend, precv, loc,
):
    group, wide, y, z, x, c = place()
    yx = y * 4 + x
    core = (group, wide_of(y, z, x, 1 - c))
    before = (group, (wide + 127) % 128)
    after = (group, (wide + 1) % 128)
    sigma = 1 - 2 * c
    ahead = (group, wide_of(y, (z + 8 + sigma) % 8, x, c))
    behind = (group, wide_of(y, (z + 8 - sigma) % 8, x, c))

    def peer(j):
        other = (yx + j) % 8
        return (group, wide_of(other // 4, z, other % 4, c))

    barrier = pltpu.get_barrier_semaphore()
    for neighbour in (ahead, behind, core, before, after):
        pl.semaphore_signal(barrier, inc=1, device_id=neighbour, device_id_type=MESH)

    def greet(j, carry):
        pl.semaphore_signal(barrier, inc=1, device_id=peer(j), device_id_type=MESH)
        return carry

    lax.fori_loop(1, 8, greet, 0)
    pl.semaphore_wait(barrier, 12)

    follow = remote(normed.at[pl.ds(0, 16)], first, fsem.at[0], fsem.at[1], before)
    follow.start()
    keep = pltpu.make_async_copy(normed, nall.at[c], loc.at[0])
    keep.start()
    swap = remote(normed, nall.at[c], nsem.at[0], nsem.at[1], core)
    swap.start()

    predicted = lax.dot_general(
        normed[...], wall[...].reshape(1024, D), (((1,), (1,)), ((), ())), preferred_element_type=F32
    )
    lanes = pl.ds(pl.multiple_of(group * UNITS, 128), UNITS)
    own = normed[:, lanes].astype(F32)
    follow.wait()
    row = iota((TOK, 1), 0)
    nearest = pltpu.roll(own, TOK - 1, 0)
    target = jnp.where(row == TOK - 1, first[:, lanes].astype(F32)[0:1, :], nearest).astype(BF16)
    target = dot(target, drafter_order((UNITS, 1024), 0, True))
    inside = (wide * TOK + row) < 128 * TOK - 1
    residual = jnp.where(inside, predicted - target, 0.0).astype(BF16)
    residual = dot(residual, drafter_order((1024, UNITS), 1, True)).astype(BF16)
    error_ref[...] = residual
    ordered = dot(residual, drafter_order((UNITS, UNITS), 0, False)).astype(BF16)
    err[0] = ordered[:, 0:384]
    err[1] = ordered[:, 384:768]
    keep_err = pltpu.make_async_copy(err.at[c], eall.at[c], loc.at[1])
    keep_err.start()
    swap_err = remote(err.at[1 - c], eall.at[c], esem.at[0], esem.at[1], core)
    swap_err.start()
    keep.wait()
    swap.wait()
    keep_err.wait()
    swap_err.wait()
    factors = eall[...].reshape(256, 384).astype(F32).T.astype(BF16)
    gsum[...] = dot(factors, nall[...].reshape(256, D)) * grad_scale

    def own_part(d):
        s = (z + 8 + d * sigma) % 8
        return gsum[pl.ds(pl.multiple_of(48 * s, 16), 48), :]

    sends = []

    def hop(buffer, k, device, n):
        copy = remote(buffer.at[k], buffer.at[k - 1], rsend.at[n, k], rrecv.at[n, k - 1], device)
        copy.start()
        sends.append(copy)

    def landed(buffer, k, n):
        remote(buffer.at[k], buffer.at[k], rsend.at[n, k], rrecv.at[n, k], ahead).wait_recv()

    maj[4] = own_part(4).astype(BF16)
    hop(maj, 4, ahead, 0)
    mnr[3] = own_part(-3).astype(BF16)
    hop(mnr, 3, behind, 1)
    for k in (3, 2, 1):
        landed(maj, k, 0)
        maj[k] = (maj[k].astype(F32) + own_part(k)).astype(BF16)
        hop(maj, k, ahead, 0)
        if k < 3:
            landed(mnr, k, 1)
            mnr[k] = (mnr[k].astype(F32) + own_part(-k)).astype(BF16)
            hop(mnr, k, behind, 1)
    landed(mnr, 0, 1)
    landed(maj, 0, 0)
    total = (own_part(0) + mnr[0].astype(F32) + maj[0].astype(F32)).astype(BF16)
    q = iota((64, 48), 0)
    expand = ((q // 8) * 6 + q % 8 == iota((64, 48), 1)) & (q % 8 < 6)
    slab[...] = dot(expand.astype(F32).astype(BF16), total).reshape(8, 8, D).astype(BF16)
    keep_fin = pltpu.make_async_copy(slab.at[yx], fin.at[yx], loc.at[2])
    keep_fin.start()

    def send(j, carry):
        remote(slab.at[(yx + j) % 8], fin.at[yx], psend, precv, peer(j)).start()
        return carry

    lax.fori_loop(1, 8, send, 0)
    keep_fin.wait()
    whole = remote(slab.at[pl.ds(0, 7)], fin.at[pl.ds(0, 7)], psend, precv, core)
    whole.wait_recv()
    gradient = jnp.sum(fin[...].astype(F32), axis=0)
    grad_ref[...] = gradient.astype(BF16)
    whole.wait_send()
    for copy in sends:
        copy.wait_send()


def params(number=None):
    if number is None:
        return pltpu.CompilerParams(vmem_limit_bytes=58 << 20)
    return pltpu.CompilerParams(vmem_limit_bytes=58 << 20, collective_id=number, has_side_effects=True)


VM = pl.BlockSpec(memory_space=pltpu.VMEM)
ANY = pl.BlockSpec(memory_space=pl.ANY)


def out(shape, kind=BF16):
    return jax.ShapeDtypeStruct(shape, kind)


def shards(
    tokens, routes, router, gate_codes, gate_scales, up_codes, up_scales, down_codes, down_scales, norm_gain,
    drafter_weight,
):
    dma = pltpu.SemaphoreType.DMA
    padded = jnp.pad(drafter_weight, ((0, 2), (0, 0)))
    block = pl.pallas_call(
        prep_kernel, out_shape=out((BLOCKS, SLOT, D)), in_specs=[VM] * 4, out_specs=VM,
        compiler_params=params(), name="prep",
    )(tokens, routes.T, router, padded)
    frame = (NZ, PLANE, SLOT, D)
    xr, wg, wu, wd, comb, wz = pl.pallas_call(
        dispatch_kernel,
        out_shape=(
            out(frame), out((D, UNITS)), out((D, UNITS)), out((UNITS, D)), out((NZ, 2, TOK, TOK)), out((NZ, SLOT, D)),
        ),
        in_specs=[VM] + [ANY] * 6,
        out_specs=(VM,) * 6,
        scratch_shapes=[
            pltpu.VMEM((NZ, BLOCKS, SLOT, D), BF16),
            pltpu.VMEM(frame, BF16),
            pltpu.VMEM((WORDS, UNITS), jnp.int32),
            pltpu.VMEM((90, UNITS), jnp.int32),
            pltpu.VMEM((WORDS, UNITS), jnp.int32),
            pltpu.VMEM((90, UNITS), jnp.int32),
            pltpu.VMEM((256, D), jnp.int32),
            pltpu.VMEM((24, D), jnp.int32),
            dma((6,)), dma((7,)), dma((7,)), dma((NZ,)), dma((NZ,)), dma((NZ,)),
        ],
        compiler_params=params(1),
        name="dispatch",
    )(
        block, gate_codes[0], gate_scales[0], up_codes[0], up_scales[0], down_codes[0], down_scales[0],
    )
    normed, wall = pl.pallas_call(
        expert_kernel,
        out_shape=(out((TOK, D)), out((2, 2, 4, NZ, SLOT, D))),
        in_specs=[VM] * 7,
        out_specs=(VM, VM),
        scratch_shapes=[
            pltpu.VMEM((1024, UNITS), BF16),
            pltpu.VMEM(frame, BF16),
            pltpu.VMEM(frame, BF16),
            pltpu.VMEM((5, TOK, D), BF16),
            pltpu.VMEM((4, TOK, D), BF16),
            pltpu.VMEM((TOK, D), BF16),
            pltpu.VMEM((TOK, D), BF16),
            dma((NZ,)), dma, dma((NZ,)), dma((NZ,)), dma((2, 5)), dma((2, 5)), dma((2,)), dma((3,)), dma((3,)),
        ],
        compiler_params=params(2),
        name="experts",
    )(xr, wg, wu, wd, comb, wz, norm_gain[None, :])
    grad_scale = 1.0 / math.sqrt(TOK * lax.axis_size("wide"))
    error, gradient = pl.pallas_call(
        functools.partial(drafter_kernel, grad_scale),
        out_shape=(out((TOK, UNITS)), out((SLOT, D))),
        in_specs=[VM] * 2,
        out_specs=(VM, VM),
        scratch_shapes=[
            pltpu.VMEM((2, TOK, D), BF16),
            pltpu.VMEM((16, D), BF16),
            pltpu.VMEM((2, TOK, 384), BF16),
            pltpu.VMEM((2, TOK, 384), BF16),
            pltpu.VMEM((384, D), F32),
            pltpu.VMEM((5, 48, D), BF16),
            pltpu.VMEM((4, 48, D), BF16),
            pltpu.VMEM((8, SLOT, D), BF16),
            pltpu.VMEM((8, SLOT, D), BF16),
            dma((2,)), dma((2,)), dma((2,)), dma((2, 5)), dma((2, 5)), dma, dma, dma((3,)),
        ],
        compiler_params=params(3),
        name="drafter",
    )(normed, wall)
    return (error, gradient[:6])


def solution(mesh):
    placed = (
        P("wide", None),
        P("wide", None),
        P(),
        P("wide", None, "group"),
        P("wide", None, "group"),
        P("wide", None, "group"),
        P("wide", None, "group"),
        P("wide", "group", None),
        P("wide", "group", None),
        P(),
        P(("group", "wide"), None),
    )
    return jax.shard_map(
        shards,
        mesh=mesh,
        in_specs=placed,
        out_specs=(P("wide", "group"), P(("group", "wide"), None)),
        check_vma=False,
    )
```

time: 1220 us -> 332 us (0.27)
  blocking collectives: 651 us -> 0 us
  waiting for transfers between devices: 329 us -> 0 us
  Pallas kernels: 0 us -> 316 us
  local copies, waits for them, and re-layouts: 113 us -> 12.5 us
  other arithmetic: 39.9 us -> 0 us
  matrix products: 32.7 us -> 0 us
  starting transfers between devices: 32.4 us -> 0 us
  between operations: 17 us -> 0.67 us
    unnamed x1 -> x0, blocking collectives: 640 us -> none
    pallas_call x0 -> x4, Pallas kernels: none -> 316 us  [the longest x1 166 us: shards(): pl.pallas_call(expert_kernel, out_shape=(out((TOK, D)), out((2, 2, 4, NZ,...]
    reduce_scatter x1 -> x0, waiting for transfers between devices: 136 us -> none  [shards(): lax.psum_scatter(outputs, 'group', scatter_dimension=2, tiled=True)]
    all_to_all x2 -> x0, waiting for transfers between devices: 120 us -> none  [the longest x1 78.3 us: shards(): lax.all_to_all(summed, 'wide', split_axis=0, concat_axis=0, tiled=True)]
    all_gather x1 -> x0, waiting for transfers between devices: 71.4 us -> none  [shards(): lax.all_gather(drafter_weight, 'wide', axis=0, tiled=True)]
    shift_right_arithmetic x11 -> x0, local copies, waits for them, and re-layouts: 69.3 us -> none  [dequantize(): nibble = packed[:, None, :] >> shifts[None, :, None] & 15]
    dot_general x6 -> x0, matrix products: 32.7 us -> none  [the longest x1 8.53 us: shards(): up_act = jnp.dot(inputs, up_w, preferred_element_type=jnp.float32)]
    all_to_all x2 -> x0, starting transfers between devices: 30.9 us -> none  [the longest x1 16.5 us: shards(): lax.all_to_all(summed, 'wide', split_axis=0, concat_axis=0, tiled=True)]
  transfers between devices with their start and end apart: 5 -> 0, of which waited for: 4 -> 0; matrix products, arithmetic and copies ran while one was open for 11% -> 0% of each run, Pallas kernels for 0% -> 0%
where the time goes in v1:
time: 332 us; the launch traced here: 329 us
  Pallas kernels  316 us (95%)
  local copies, waits for them, and re-layouts  12.5 us (4%)
    pallas_call x1, Pallas kernels, shards(): pl.pallas_call(expert_kernel, out_shape=(out((TOK, D)), out((2, 2, 4, NZ,...  166 us
    pallas_call x1, Pallas kernels, shards(): pl.pallas_call(dispatch_kernel, out_shape=(out(frame), out((D, UNITS)), o...  98 us
    pallas_call x1, Pallas kernels, shards(): pl.pallas_call(functools.partial(drafter_kernel, grad_scale), out_shape=(...  49.2 us
    unnamed x7, local copies, waits for them, and re-layouts  9.66 us

profile of v1, /device:TPU:16, one launch (start us, length us, event | category | flops | bytes accessed | tf_op | source)
XLA Modules:
  0.0 329.2 jit_solution(5295037305783977648)
XLA Ops:
  0.6 0.0 copy-start
  0.6 1.5 broadcast_in_dim.3.gain
  2.1 1.4 pad.4.weight_ref
  3.5 2.0 copy_bitcast_fusion
  5.5 2.3 copy.13.tokens_ref
  7.8 3.1 prep.1.blk
  10.9 0.0 copy-done
  10.9 2.4 copy.14
  13.3 98.0 %dispatch.1 = (bf16[8,16,8,2880]{3,2,1,0:T(8,128)(2,1)}, bf16[2880,768]{1,0:T(8,128)(2,1)}, bf16[2880,768]{1,0:T(8,128)(2,1)}, bf16[768,2880]{1,0:T(8,128)(2,1)}...) custom-call(bf16[17,8,2880]{2,1,0:T(8,128)(2,1)} %prep.1.blk, s32[960,768]{1,0:T(8,128)} %bitcast.11, ...), custom_call_target="tpu_custom_call" | custom-call | tf_op jit(solution)/shard_map/dispatch/pallas_call | solution.py:551
  111.3 165.6 %experts.1 = (bf16[128,2880]{1,0:T(8,128)(2,1)}, bf16[2,2,4,8,8,2880]{5,4,3,2,1,0:T(8,128)(2,1)}) custom-call(bf16[8,16,8,2880]{3,2,1,0:T(8,128)(2,1)} %get-tuple-element.12.xr, bf16[2880,768]{1,0:T(8,128)(2,1)} %get-tuple-element.13.wg, bf16[2880,768]{1,0:T(8,128)(2,1)} %get-tuple-element.14.wu, bf16[768,2880]{1,0:T(8,128)(2,1)} %get-tuple-element.15.wd, ...), custom_call_target="tpu_custom_call" | custom-call | tf_op jit(solution)/shard_map/experts/pallas_call | solution.py:574
  276.9 49.2 %drafter.1 = (bf16[128,768]{1,0:T(8,128)(2,1)}, bf16[8,2880]{1,0:T(8,128)(2,1)}) custom-call(bf16[128,2880]{1,0:T(8,128)(2,1)} %get-tuple-element.18.normed, bf16[2,2,4,8,8,2880]{5,4,3,2,1,0:T(8,128)(2,1)} %get-tuple-element.19.wall), custom_call_target="tpu_custom_call" | custom-call | tf_op jit(solution)/shard_map/drafter/pallas_call | solution.py:593
  326.1 1.6 copy.21
  327.7 1.4 copy.22
Async XLA Ops:
  0.6 10.3 %copy-start = (s32[1,256,2880]{1,2,0:T(8,128)S(1)}, s32[1,256,2880]{1,2,0:T(8,128)}, u32[]{:S(2)}) copy-start(s32[1,256,2880]{1,2,0:T(8,128)} %param.18) | copy-start | bytes 8847364

commit v2 on v0

v2 whole, which is shorter than its diff:
```python
import functools
import math

import jax
import jax.numpy as jnp
from jax import lax
from jax.experimental import pallas as pl
from jax.experimental.pallas import tpu as pltpu
from jax.sharding import PartitionSpec as P

MESH = pl.DeviceIdType.MESH
F32 = jnp.float32
BF16 = jnp.bfloat16

D = 2880
TOK = 128
NZ = 8
PLANE = 16
SLOT = 8
SLABS = TOK // SLOT
UNITS = 768
WORDS = 960
BLOCKS = SLABS + 1
META = 6


def place():
    group, wide = lax.axis_index("group"), lax.axis_index("wide")
    y, z, x, c = wide // 64, (wide // 8) % 8, (wide // 2) % 4, wide % 2
    return group, wide, y, z, x, c


def wide_of(y, z, x, c):
    return y * 64 + z * 8 + x * 2 + c


def plane_wide(p, z):
    return (p // 8) * 64 + z * 8 + p % 8


def iota(shape, dim, kind=jnp.int32):
    return lax.broadcasted_iota(jnp.int32, shape, dim).astype(kind)


def dot(a, b):
    return jnp.dot(a, b, preferred_element_type=F32)


def dot_first(a, b):
    return lax.dot_general(a, b, (((0,), (0,)), ((), ())), preferred_element_type=F32)


def remote(src, dst, send, recv, device):
    return pltpu.make_async_remote_copy(
        src_ref=src, dst_ref=dst, send_sem=send, recv_sem=recv, device_id=device, device_id_type=MESH
    )


def spread(columns):
    parts = []
    for start, length in [(384 * b, 384) for b in range(7)] + [(2688, 192)]:
        third = length // 3
        row = iota((length, length), 0)
        column = iota((length, length), 1)
        order = (row == 3 * (column % third) + column // third).astype(F32).astype(BF16)
        parts.append(dot_first(columns[start : start + length, :], order).astype(BF16))
    return parts


def level(nibble):
    m = nibble & 7
    twice = m + jnp.maximum(m - 4, 0) + 2 * jnp.maximum(m - 6, 0)
    return twice.astype(F32)


def unpack(words, j, scales):
    nibble = (words >> (4 * j)) & 15
    half = jnp.exp2((scales - 1).astype(F32))
    return level(nibble) * jnp.where(nibble >= 8, -half, half)


def scale_rows(ref, q, j, width):
    r = iota((32, width), 0)
    block = (3 * r + j) // 32
    rows = [ref[3 * q + n] if len(ref.shape) == 3 else ref[pl.ds(3 * q + n, 1), :] for n in range(3)]
    return jnp.where(block == 0, rows[0], jnp.where(block == 1, rows[1], rows[2]))


def dequant_in(codes, scales, out, q, base, third):
    words = codes[pl.ds(pl.multiple_of(32 * q, 32), 32), :]
    for j in range(3):
        values = unpack(words, j, scale_rows(scales, q, j, words.shape[1]))
        out[pl.ds(pl.multiple_of(base + third * j, 32), 32), :] = values.astype(BF16)


def dequant_wide(codes, scales, out, first, last):
    def step(q, carry):
        dequant_in(codes, scales, out, q, (q // 4) * 384 + (q % 4) * 32, 128)
        return carry

    lax.fori_loop(first, min(last, 28), step, 0)
    for q in range(28, last):
        dequant_in(codes, scales, out, q, 2688 + (q - 28) * 32, 64)


def layer_kernel(
    tokens_ref, routes_ref, router_ref, drafter_ref, gain, gc, gs, uc, us, dc, ds, normed_ref, wall,
    tokv, routev, routerv, agb, snd, xr, ret, wide_codes, wide_scales, dcv, dsv, wg, wu, wd, comb, wz, hid,
    maj, mnr, sall, in_sem, code_sem, zsend, zrecv, psend, precv, loc, qsend, qrecv, qloc,
    rsend, rrecv, xsend, xrecv, wsend, wrecv, wloc,
):
    group, wide, y, z, x, c = place()
    p_me = y * 8 + x * 2 + c
    sigma = 1 - 2 * c
    y4 = 2 * group + y

    def along_y(n):
        place_y = (y4 + n) % 4
        return (place_y // 2, wide_of(place_y % 2, z, x, c))

    core = (group, wide_of(y, z, x, 1 - c))
    right = (group, wide_of(y, (z + 1) % 8, x, c))
    left = (group, wide_of(y, (z + 7) % 8, x, c))
    ahead = (group, wide_of(y, (z + 8 + sigma) % 8, x, c))
    behind = (group, wide_of(y, (z + 8 - sigma) % 8, x, c))

    loads = [
        pltpu.make_async_copy(a, b, in_sem.at[n])
        for n, (a, b) in enumerate([(tokens_ref, tokv), (routes_ref, routev), (router_ref, routerv)])
    ]
    gate_codes = pltpu.make_async_copy(gc, wide_codes, code_sem.at[0])
    gate_scales = pltpu.make_async_copy(gs, wide_scales, code_sem.at[1])
    up_codes = pltpu.make_async_copy(uc, wide_codes, code_sem.at[2])
    up_scales = pltpu.make_async_copy(us, wide_scales, code_sem.at[3])
    down_codes = pltpu.make_async_copy(dc, dcv, code_sem.at[4])
    down_scales = pltpu.make_async_copy(ds, dsv, code_sem.at[5])
    for copy in loads + [gate_codes, gate_scales, down_codes, down_scales]:
        copy.start()

    barrier = pltpu.get_barrier_semaphore()
    for neighbour in (left, right, along_y(1), along_y(3)):
        pl.semaphore_signal(barrier, inc=1, device_id=neighbour, device_id_type=MESH)

    def greet(j, carry):
        p = (p_me + j) % PLANE
        pl.semaphore_signal(barrier, inc=1, device_id=(group, plane_wide(p, z)), device_id_type=MESH)
        return carry

    lax.fori_loop(1, PLANE, greet, 0)

    def greet_other(j, carry):
        p = (1 - y) * 8 + j
        pl.semaphore_signal(barrier, inc=1, device_id=(1 - group, plane_wide(p, z)), device_id_type=MESH)
        return carry

    lax.fori_loop(0, 8, greet_other, 0)

    for copy in loads:
        copy.wait()
    columns = tokv[...]
    column = 0
    for part in spread(columns):
        width = part.shape[1]
        agb[z, 0:SLABS, :, column : column + width] = part.astype(F32).reshape(SLABS, SLOT, width).astype(BF16)
        column += width
    weight = jax.nn.sigmoid(dot_first(routerv[...], columns))
    named_expert = iota((TOK, TOK), 0)
    routes, high, low = [], [], []
    for k in range(4):
        route = routev[k : k + 1, :]
        chosen = jnp.sum(jnp.where(named_expert == route, weight, 0.0), axis=0, keepdims=True)
        top = chosen.astype(BF16).astype(F32)
        routes.append(route.astype(F32))
        high.append(top)
        low.append(chosen - top)
    line = jnp.concatenate(routes + high + low + [jnp.zeros((1, D - 12 * TOK), F32)], axis=1)
    drafter = jnp.concatenate([drafter_ref[...].astype(F32), line, jnp.zeros((1, D), F32)], axis=0)
    agb[z, SLABS] = drafter.astype(BF16)
    pl.semaphore_wait(barrier, 27)

    sends = []
    halves = (pl.ds(0, 9), pl.ds(9, 8))

    def forward(s, part, device, n):
        ref = agb.at[s, halves[part]]
        copy = remote(ref, ref, zsend.at[n, part], zrecv.at[n, part], device)
        copy.start()
        sends.append(copy)

    def arrived(s, part, n):
        ref = agb.at[s, halves[part]]
        remote(ref, ref, zsend.at[n, part], zrecv.at[n, part], right).wait_recv()

    upper = (iota((TOK, TOK), 0) < iota((TOK, TOK), 1)).astype(F32).astype(BF16)
    p_rows = iota((PLANE, 1), 0)
    experts = ((p_rows // 8) * 64 + z * 8 + p_rows % 8).astype(F32)

    def plane_send(target, s, send_sem, recv_sem):
        def send(j, carry):
            p = (p_me + j) % PLANE
            across = ((p // 8 + y) % 2) * (s % 2)
            remote(
                snd.at[s, p], target.at[s, p_me], send_sem.at[s], recv_sem.at[s],
                ((group + across) % 2, plane_wide(p, z)),
            ).start()
            return carry

        lax.fori_loop(1, PLANE, send, 0)

    def plane_copies(target, s, send_sem, recv_sem):
        return remote(snd.at[s, pl.ds(0, 15)], target.at[s, pl.ds(0, 15)], send_sem.at[s], recv_sem.at[s], core)

    def relay(s):
        meta = agb[s, SLABS, :, 0 : 12 * TOK].astype(F32)[META : META + 1, :]
        named = jnp.zeros((PLANE, TOK), F32)
        weight = jnp.zeros((PLANE, TOK), F32)
        for k in range(4):
            hit = (experts == meta[:, k * TOK : (k + 1) * TOK]).astype(F32)
            value = meta[:, (4 + k) * TOK : (5 + k) * TOK] + meta[:, (8 + k) * TOK : (9 + k) * TOK]
            named = named + hit
            weight = weight + hit * value
        rank = dot(named.astype(BF16), upper)
        slot = iota((PLANE, SLOT, TOK), 1, F32)
        pick = jnp.where(rank[:, None, :] == slot, named[:, None, :], 0.0)
        rows = dot(pick.reshape(TOK, TOK).astype(BF16), agb[s, 0:SLABS].reshape(TOK, D))
        snd[s] = rows.reshape(PLANE, SLOT, D).astype(BF16)
        pltpu.make_async_copy(snd.at[s, p_me], xr.at[s, p_me], loc.at[s]).start()
        plane_send(xr, s, psend, precv)
        weighted = (pick * weight[:, None, :]).reshape(TOK, TOK).T
        top = weighted.astype(BF16)
        comb[s, 0] = top
        comb[s, 1] = (weighted - top.astype(F32)).astype(BF16)
        wz[s] = agb[s, SLABS]

    def source(d):
        return (z + 8 + d * sigma) % 8

    order_row = iota((UNITS, UNITS), 0)
    order_column = iota((UNITS, UNITS), 1)

    def experts_on(*distances):
        inputs = []
        for d in distances:
            s = source(d)
            pltpu.make_async_copy(snd.at[s, p_me], xr.at[s, p_me], loc.at[s]).wait()
            plane_copies(xr, s, psend, precv).wait_recv()
            inputs.append(xr[s].reshape(TOK, D))
        inputs = jnp.concatenate(inputs, axis=0)
        act = (jax.nn.silu(dot(inputs, wg[...])) * dot(inputs, wu[...])).astype(BF16)
        order = (order_row == 3 * (order_column % 256) + order_column // 256).astype(F32).astype(BF16)
        act = dot(act, order).astype(BF16)
        for n, d in enumerate(distances):
            hid[pl.ds(pl.multiple_of(TOK * source(d), TOK), TOK), :] = act[n * TOK : (n + 1) * TOK]

    def dequant_down(first, last):
        def step(q, carry):
            words = dcv[pl.ds(pl.multiple_of(32 * q, 32), 32), :]
            for j in range(3):
                values = unpack(words, j, scale_rows(dsv, q, j, D))
                wd[pl.ds(pl.multiple_of(256 * j + 32 * q, 32), 32), :] = values.astype(BF16)
            return carry

        lax.fori_loop(first, last, step, 0)

    def beside(n):
        if n == 0:
            gate_codes.wait()
            gate_scales.wait()
            dequant_wide(wide_codes, wide_scales, wg, 0, 16)
        elif n == 1:
            dequant_wide(wide_codes, wide_scales, wg, 16, 30)
            up_codes.start()
            up_scales.start()
        elif n == 2:
            down_codes.wait()
            down_scales.wait()
            dequant_down(0, 4)
        elif n == 3:
            dequant_down(4, 8)
        elif n == 4:
            up_codes.wait()
            up_scales.wait()
            dequant_wide(wide_codes, wide_scales, wu, 0, 14)
        elif n == 5:
            dequant_wide(wide_codes, wide_scales, wu, 14, 30)

    for part in range(2):
        forward(z, part, right, 0)
        forward(z, part, left, 1)
    relay(z)
    beside(0)
    for k in (1, 2, 3):
        back, front = (z + 8 - k) % 8, (z + k) % 8
        far = (z + 8 - 3 * sigma) % 8
        for part in range(2):
            arrived(back, part, 2 * k - 2)
            if k < 3:
                forward(back, part, right, 2 * k)
            arrived(front, part, 2 * k - 1)
            if k < 3:
                forward(front, part, left, 2 * k + 1)
            else:
                forward(far, part, ahead, 6)
            if part == 0:
                beside(2 * k - 1)
        relay(back)
        relay(front)
        beside(2 * k)
    experts_on(0, 1)
    opposite = (z + 4) % 8
    arrived(opposite, 0, 6)
    arrived(opposite, 1, 6)
    relay(opposite)
    experts_on(-1, 2)
    experts_on(-2, 3)
    experts_on(-3)
    experts_on(4)

    def down(d):
        s = source(d)
        plane_copies(xr, s, psend, precv).wait_send()
        rows = dot(hid[pl.ds(pl.multiple_of(TOK * s, TOK), TOK), :], wd[...])
        snd[s] = rows.reshape(PLANE, SLOT, D).astype(BF16)
        pltpu.make_async_copy(snd.at[s, p_me], ret.at[s, p_me], qloc.at[s]).start()
        plane_send(ret, s, qsend, qrecv)

    def combined(d):
        s = source(d)
        pltpu.make_async_copy(snd.at[s, p_me], ret.at[s, p_me], qloc.at[s]).wait()
        plane_copies(ret, s, qsend, qrecv).wait_recv()
        rows = ret[s].reshape(TOK, D)
        return dot(comb[s, 0], rows) + dot(comb[s, 1], rows)

    half_rows = (pl.ds(0, 64), pl.ds(64, 64))

    def hop(buffer, k, half, device, n):
        copy = remote(
            buffer.at[k, half_rows[half]], buffer.at[k - 1, half_rows[half]],
            rsend.at[n, k, half], rrecv.at[n, k - 1, half], device,
        )
        copy.start()
        sends.append(copy)

    def landed(buffer, k, half, n):
        ref = buffer.at[k, half_rows[half]]
        remote(ref, ref, rsend.at[n, k, half], rrecv.at[n, k, half], ahead).wait_recv()

    def join(buffer, k, half, part, device, n):
        landed(buffer, k, half, n)
        rows = half_rows[half]
        buffer[k, rows] = (buffer[k, rows].astype(F32) + part[64 * half : 64 * half + 64]).astype(BF16)
        hop(buffer, k, half, device, n)

    down(4)
    down(3)
    down(-3)
    maj[4] = combined(4).astype(BF16)
    hop(maj, 4, 0, ahead, 0)
    hop(maj, 4, 1, ahead, 0)
    down(2)
    down(-2)
    mnr[3] = combined(-3).astype(BF16)
    hop(mnr, 3, 0, behind, 1)
    hop(mnr, 3, 1, behind, 1)
    part = combined(3)
    join(maj, 3, 0, part, ahead, 0)
    join(maj, 3, 1, part, ahead, 0)
    down(1)
    down(-1)
    part, minor = combined(2), combined(-2)
    for half in range(2):
        join(mnr, 2, half, minor, behind, 1)
        join(maj, 2, half, part, ahead, 0)
    down(0)

    keep = pltpu.make_async_copy(wz, wall.at[x], wloc)
    keep.start()

    def share_x(j, carry):
        remote(wz, wall.at[x], wsend, wrecv, (group, wide_of(y, z, (x + j) % 4, c))).start()
        return carry

    lax.fori_loop(1, 4, share_x, 0)

    part, minor = combined(1), combined(-1)
    for half in range(2):
        join(mnr, 1, half, minor, behind, 1)
        join(maj, 1, half, part, ahead, 0)
    part = combined(0)

    def pass_y(owner, half, step, n):
        ref = sall.at[owner, half_rows[half]]
        copy = remote(ref, ref, xsend.at[n, half], xrecv.at[n, half], along_y(step))
        copy.start()
        sends.append(copy)

    def got_y(owner, half, n):
        ref = sall.at[owner, half_rows[half]]
        remote(ref, ref, xsend.at[n, half], xrecv.at[n, half], core).wait_recv()

    below, above, across_y = (y4 + 3) % 4, (y4 + 1) % 4, (y4 + 2) % 4
    for half, rows in enumerate(half_rows):
        landed(mnr, 0, half, 1)
        landed(maj, 0, half, 0)
        total = part[64 * half : 64 * half + 64] + mnr[0, rows].astype(F32) + maj[0, rows].astype(F32)
        sall[y4, rows] = total.astype(BF16)
        pass_y(y4, half, 1, 0)
        pass_y(y4, half, 3, 1)
    got_y(below, 0, 0)
    pass_y(below, 0, 1, 2)
    got_y(above, 1, 1)
    pass_y(above, 1, 3, 2)
    got_y(below, 1, 0)
    got_y(above, 0, 1)
    for half, rows in enumerate(half_rows):
        got_y(across_y, half, 2)
        for q in range(2):
            feature = (sall[q, rows].astype(F32) + sall[q + 2, rows].astype(F32)).astype(BF16).astype(F32)
            mean_square = jnp.sum(feature * feature, axis=1, keepdims=True) / D
            normed_ref[q, rows] = (feature * lax.rsqrt(mean_square + 1e-05) * gain[...]).astype(BF16)
    for copy in sends:
        copy.wait_send()
    for s in range(NZ):
        plane_copies(ret, s, qsend, qrecv).wait_send()
    keep.wait()
    three = remote(wall.at[pl.ds(0, 3)], wall.at[pl.ds(0, 3)], wsend, wrecv, core)
    three.wait()


def drafter_kernel(
    grad_scale, normed, wall, error_ref, grad_ref,
    nall, first, err, eall, gsum, maj, mnr, slab, fin, fsem, nsem, esem, rsend, rrecv, psend, precv, loc,
):
    group, wide, y, z, x, c = place()
    core = (group, wide_of(y, z, x, 1 - c))
    chip = z * 4 + x
    before, after = (chip + 31) % 32, (chip + 1) % 32
    before = (group, wide_of(y, before // 4, before % 4, c))
    after = (group, wide_of(y, after // 4, after % 4, c))
    sigma = 1 - 2 * c
    ahead = (group, wide_of(y, (z + 8 + sigma) % 8, x, c))
    behind = (group, wide_of(y, (z + 8 - sigma) % 8, x, c))
    me = y * 2 + c

    def mate(j):
        n = (me + j) % 4
        return (group, wide_of(n // 2, z, x, n % 2))

    def peer(j):
        return (group, wide_of(y, z, (x + j) % 4, c))

    barrier = pltpu.get_barrier_semaphore()
    for neighbour in (ahead, behind, before, after, mate(1), mate(2), mate(3), peer(1), peer(2), peer(3)):
        pl.semaphore_signal(barrier, inc=1, device_id=neighbour, device_id_type=MESH)
    pl.semaphore_wait(barrier, 10)

    keep = pltpu.make_async_copy(normed, nall.at[c], loc.at[0])
    keep.start()
    swap = remote(normed, nall.at[c], nsem.at[0], nsem.at[1], core)
    swap.start()
    lanes = pl.ds(pl.multiple_of(group * UNITS, 128), UNITS)
    keep.wait()
    swap.wait()
    follow = remote(nall.at[0, :, pl.ds(0, 16), lanes], first, fsem.at[0], fsem.at[1], before)
    follow.start()
    predicted = lax.dot_general(
        nall[...].reshape(512, D), wall[...].reshape(256, D), (((1,), (1,)), ((), ())), preferred_element_type=F32
    )
    follow.wait()

    feature, column = iota((UNITS, 256), 0), iota((UNITS, 256), 1)
    x_of, z_of, i_of = column // 64, (column // 8) % 8, column % 8
    choose = ((feature == y * 384 + z_of * 48 + x_of * 12 + c * 6 + i_of) & (i_of < 6)).astype(F32).astype(BF16)
    row = iota((TOK, 1), 0)
    last_chip = chip == 31
    for core_of in range(2):
        for y_of in range(2):
            own = nall[core_of, y_of, :, lanes].astype(F32)
            if core_of == 0:
                following = nall[1, y_of, 0:16, lanes].astype(F32)[0:1, :]
            else:
                following = jnp.where(last_chip, first[1 - y_of].astype(F32)[0:1, :], first[y_of].astype(F32)[0:1, :])
            target = jnp.where(row == TOK - 1, following, pltpu.roll(own, TOK - 1, 0)).astype(BF16)
            start = (core_of * 2 + y_of) * TOK
            residual = predicted[start : start + TOK] - dot(target, choose)
            position = wide_of(y_of, z, x, core_of) * TOK + row
            residual = jnp.where(position < 128 * TOK - 1, residual, 0.0).astype(BF16)
            err[y_of * 2 + core_of] = residual
    keep_err = pltpu.make_async_copy(err.at[me], eall.at[me], loc.at[1])
    keep_err.start()

    def send_err(j, carry):
        n = (me + j) % 4
        remote(
            err.at[n], eall.at[me], esem.at[0], esem.at[1], (group, wide_of(n // 2, z, x, n % 2))
        ).start()
        return carry

    lax.fori_loop(1, 4, send_err, 0)

    before_order, after_order = iota((256, 192), 0), iota((256, 192), 1)
    matched = before_order == (after_order // 6 % 4) * 64 + (after_order // 24) * 8 + after_order % 6
    compact = matched.astype(F32).astype(BF16)
    factors = []
    for core_of in range(2):
        for y_of in range(2):
            factors.append(dot(err[y_of * 2 + core_of], compact).T)
    factors = jnp.concatenate(factors, axis=1).astype(BF16)
    gsum[...] = dot(factors, nall[...].reshape(512, D)) * grad_scale

    def own_part(d):
        s = (z + 8 + d * sigma) % 8
        return gsum[pl.ds(pl.multiple_of(24 * s, 8), 24), :].reshape(3, SLOT, D)

    sends = []

    def hop(buffer, k, device, n):
        copy = remote(buffer.at[k], buffer.at[k - 1], rsend.at[n, k], rrecv.at[n, k - 1], device)
        copy.start()
        sends.append(copy)

    def landed(buffer, k, n):
        remote(buffer.at[k], buffer.at[k], rsend.at[n, k], rrecv.at[n, k], ahead).wait_recv()

    maj[4] = own_part(4).astype(BF16)
    hop(maj, 4, ahead, 0)
    mnr[3] = own_part(-3).astype(BF16)
    hop(mnr, 3, behind, 1)

    keep_err.wait()
    others = remote(err.at[pl.ds(0, 3)], eall.at[pl.ds(0, 3)], esem.at[0], esem.at[1], core)
    others.wait()
    mixed, where_to = iota((1024, UNITS), 0), iota((1024, UNITS), 1)
    i_of, z_of, x_of, n_of = mixed % 8, (mixed // 8) % 8, (mixed // 64) % 4, mixed // 256
    matched = where_to == (n_of // 2) * 384 + z_of * 48 + x_of * 12 + (n_of % 2) * 6 + i_of
    restore = (matched & (i_of < 6)).astype(F32).astype(BF16)
    every = jnp.concatenate([eall[n] for n in range(4)], axis=1)
    error_ref[...] = dot(every, restore).astype(BF16)

    for k in (3, 2, 1):
        landed(maj, k, 0)
        maj[k] = (maj[k].astype(F32) + own_part(k)).astype(BF16)
        hop(maj, k, ahead, 0)
        if k < 3:
            landed(mnr, k, 1)
            mnr[k] = (mnr[k].astype(F32) + own_part(-k)).astype(BF16)
            hop(mnr, k, behind, 1)
    landed(mnr, 0, 1)
    landed(maj, 0, 0)
    total = own_part(0) + mnr[0].astype(F32) + maj[0].astype(F32)
    total = total.reshape(24, D).astype(BF16)
    q, r = iota((32, 24), 0), iota((32, 24), 1)
    expand = ((q // 8) * 6 + q % 8 == r) & (q % 8 < 6)
    slab[...] = dot(expand.astype(F32).astype(BF16), total).reshape(4, SLOT, D).astype(BF16)
    keep_fin = pltpu.make_async_copy(slab.at[x], fin.at[x], loc.at[2])
    keep_fin.start()

    def send(j, carry):
        n = (x + j) % 4
        remote(slab.at[n], fin.at[x], psend, precv, (group, wide_of(y, z, n, c))).start()
        return carry

    lax.fori_loop(1, 4, send, 0)
    keep_fin.wait()
    whole = remote(slab.at[pl.ds(0, 3)], fin.at[pl.ds(0, 3)], psend, precv, core)
    whole.wait_recv()
    grad_ref[...] = jnp.sum(fin[...].astype(F32), axis=0).astype(BF16)
    whole.wait_send()
    for copy in sends:
        copy.wait_send()


def params(number=None):
    if number is None:
        return pltpu.CompilerParams(vmem_limit_bytes=62 << 20)
    return pltpu.CompilerParams(vmem_limit_bytes=62 << 20, collective_id=number, has_side_effects=True)


VM = pl.BlockSpec(memory_space=pltpu.VMEM)
ANY = pl.BlockSpec(memory_space=pl.ANY)


def out(shape, kind=BF16):
    return jax.ShapeDtypeStruct(shape, kind)


def shards(
    tokens, routes, router, gate_codes, gate_scales, up_codes, up_scales, down_codes, down_scales, norm_gain,
    drafter_weight,
):
    dma = pltpu.SemaphoreType.DMA
    frame = (NZ, PLANE, SLOT, D)
    normed, wall = pl.pallas_call(
        layer_kernel,
        out_shape=(out((2, TOK, D)), out((4, NZ, SLOT, D))),
        in_specs=[ANY] * 3 + [VM] * 2 + [ANY] * 6,
        out_specs=(VM, ANY),
        scratch_shapes=[
            pltpu.VMEM((D, TOK), BF16),
            pltpu.VMEM((4, TOK), jnp.int32),
            pltpu.VMEM((D, TOK), BF16),
            pltpu.VMEM((NZ, BLOCKS, SLOT, D), BF16),
            pltpu.VMEM(frame, BF16),
            pltpu.VMEM(frame, BF16),
            pltpu.VMEM(frame, BF16),
            pltpu.VMEM((WORDS, UNITS), jnp.int32),
            pltpu.VMEM((90, 1, UNITS), jnp.int32),
            pltpu.VMEM((256, D), jnp.int32),
            pltpu.VMEM((24, D), jnp.int32),
            pltpu.VMEM((D, UNITS), BF16),
            pltpu.VMEM((D, UNITS), BF16),
            pltpu.VMEM((UNITS, D), BF16),
            pltpu.VMEM((NZ, 2, TOK, TOK), BF16),
            pltpu.VMEM((NZ, SLOT, D), BF16),
            pltpu.VMEM((1024, UNITS), BF16),
            pltpu.VMEM((5, TOK, D), BF16),
            pltpu.VMEM((4, TOK, D), BF16),
            pltpu.VMEM((4, TOK, D), BF16),
            dma((3,)), dma((6,)), dma((7, 2)), dma((7, 2)), dma((NZ,)), dma((NZ,)), dma((NZ,)),
            dma((NZ,)), dma((NZ,)), dma((NZ,)), dma((2, 5, 2)), dma((2, 5, 2)), dma((3, 2)), dma((3, 2)),
            dma, dma, dma,
        ],
        compiler_params=params(1),
        name="layer",
    )(
        tokens.T, routes.T, router, drafter_weight, norm_gain[None, :], gate_codes[0],
        gate_scales.transpose(1, 0, 2), up_codes[0], up_scales.transpose(1, 0, 2), down_codes[0], down_scales[0],
    )
    grad_scale = 1.0 / math.sqrt(TOK * lax.axis_size("wide"))
    error, gradient = pl.pallas_call(
        functools.partial(drafter_kernel, grad_scale),
        out_shape=(out((TOK, UNITS)), out((SLOT, D))),
        in_specs=[VM] * 2,
        out_specs=(VM, VM),
        scratch_shapes=[
            pltpu.VMEM((2, 2, TOK, D), BF16),
            pltpu.VMEM((2, 16, UNITS), BF16),
            pltpu.VMEM((4, TOK, 256), BF16),
            pltpu.VMEM((4, TOK, 256), BF16),
            pltpu.VMEM((192, D), F32),
            pltpu.VMEM((5, 3, SLOT, D), BF16),
            pltpu.VMEM((4, 3, SLOT, D), BF16),
            pltpu.VMEM((4, SLOT, D), BF16),
            pltpu.VMEM((4, SLOT, D), BF16),
            dma((2,)), dma((2,)), dma((2,)), dma((2, 5)), dma((2, 5)), dma, dma, dma((3,)),
        ],
        compiler_params=params(2),
        name="drafter",
    )(normed, wall)
    return (error, gradient[:6])


def solution(mesh):
    placed = (
        P("wide", None),
        P("wide", None),
        P(),
        P("wide", None, "group"),
        P("wide", None, "group"),
        P("wide", None, "group"),
        P("wide", None, "group"),
        P("wide", "group", None),
        P("wide", "group", None),
        P(),
        P(("group", "wide"), None),
    )
    return jax.shard_map(
        shards,
        mesh=mesh,
        in_specs=placed,
        out_specs=(P("wide", "group"), P(("group", "wide"), None)),
        check_vma=False,
    )
```

time: 1220 us -> 249 us (0.20)
  blocking collectives: 651 us -> 0 us
  waiting for transfers between devices: 329 us -> 0 us
  Pallas kernels: 0 us -> 240 us
  local copies, waits for them, and re-layouts: 113 us -> 7.81 us
  other arithmetic: 39.9 us -> 0 us
  matrix products: 32.7 us -> 0 us
  starting transfers between devices: 32.4 us -> 0 us
  between operations: 17 us -> 0.65 us
    unnamed x1 -> x0, blocking collectives: 640 us -> none
    pallas_call x0 -> x2, Pallas kernels: none -> 240 us  [the longest x1 199 us: shards(): pl.pallas_call(layer_kernel, out_shape=(out((2, TOK, D)), out((4, NZ, SLO...]
    reduce_scatter x1 -> x0, waiting for transfers between devices: 136 us -> none  [shards(): lax.psum_scatter(outputs, 'group', scatter_dimension=2, tiled=True)]
    all_to_all x2 -> x0, waiting for transfers between devices: 120 us -> none  [the longest x1 78.3 us: shards(): lax.all_to_all(summed, 'wide', split_axis=0, concat_axis=0, tiled=True)]
    all_gather x1 -> x0, waiting for transfers between devices: 71.4 us -> none  [shards(): lax.all_gather(drafter_weight, 'wide', axis=0, tiled=True)]
    shift_right_arithmetic x11 -> x0, local copies, waits for them, and re-layouts: 69.3 us -> none  [dequantize(): nibble = packed[:, None, :] >> shifts[None, :, None] & 15]
    dot_general x6 -> x0, matrix products: 32.7 us -> none  [the longest x1 8.53 us: shards(): up_act = jnp.dot(inputs, up_w, preferred_element_type=jnp.float32)]
    all_to_all x2 -> x0, starting transfers between devices: 30.9 us -> none  [the longest x1 16.5 us: shards(): lax.all_to_all(summed, 'wide', split_axis=0, concat_axis=0, tiled=True)]
  transfers between devices with their start and end apart: 5 -> 0, of which waited for: 4 -> 0; matrix products, arithmetic and copies ran while one was open for 11% -> 0% of each run, Pallas kernels for 0% -> 0%
where the time goes in v2:
time: 249 us
  Pallas kernels  240 us (96%)
  local copies, waits for them, and re-layouts  7.81 us (3%)
    pallas_call x1, Pallas kernels, shards(): pl.pallas_call(layer_kernel, out_shape=(out((2, TOK, D)), out((4, NZ, SLO...  199 us
    pallas_call x1, Pallas kernels, shards(): pl.pallas_call(functools.partial(drafter_kernel, grad_scale), out_shape=(...  41.4 us
    unnamed x3, local copies, waits for them, and re-layouts  6.5 us

profile of v2, /device:TPU:16, one launch (start us, length us, event | category | flops | bytes accessed | tf_op | source)
XLA Modules:
  0.0 248.7 jit_solution(7944411246598870240)
XLA Ops:
  0.6 1.3 broadcast_in_dim.3.gain
  1.9 3.5 %copy.13 = s32[1,256,2880]{2,1,0:T(8,128)} copy(s32[1,256,2880]{1,2,0:T(8,128)} %param.18) | data formatting | bytes 5898240 | tf_op args[7]
  5.4 198.8 %layer.1 = (bf16[2,128,2880]{2,1,0:T(8,128)(2,1)}, bf16[4,8,8,2880]{3,2,1,0:T(8,128)(2,1)}) custom-call(bf16[2880,128]{1,0:T(8,128)(2,1)} %bitcast.12, s32[4,128]{1,0:T(4,128)} %bitcast.17, bf16[2880,128]{1,0:T(8,128)(2,1)} %router_ref.1, bf16[6,2880]{1,0:T(8,128)(2,1)} %drafter_ref.1, f32[1,2880]{1,0:T(1,128)} %broadcast_in_dim.3.gain, ...), custom_call_target="tpu_custom_call" | custom-call | tf_op jit(solution)/shard_map/layer/pallas_call | solution.py:593
  204.3 41.4 %drafter.1 = (bf16[128,768]{1,0:T(8,128)(2,1)}, bf16[8,2880]{1,0:T(8,128)(2,1)}) custom-call(bf16[2,128,2880]{2,1,0:T(8,128)(2,1)} %get-tuple-element.6.normed, bf16[4,8,8,2880]{3,2,1,0:T(8,128)(2,1)} %get-tuple-element.7.wall), custom_call_target="tpu_custom_call" | custom-call | tf_op jit(solution)/shard_map/drafter/pallas_call | solution.py:630
  245.7 1.6 copy.16
  247.3 1.4 copy.17

commit v3 on v2

--- a/solution.py
+++ b/solution.py
@@ -18,10 +18,10 @@
 PLANE = 16
 SLOT = 8
 SLABS = TOK // SLOT
+HALF = D // 2
+ALL = 2 * PLANE
 UNITS = 768
 WORDS = 960
-BLOCKS = SLABS + 1
-META = 6
 
 
 def place():
@@ -58,7 +58,7 @@
 
 def spread(columns):
     parts = []
-    for start, length in [(384 * b, 384) for b in range(7)] + [(2688, 192)]:
+    for start, length in [(0, 384), (384, 384), (768, 384), (1152, 288)]:
         third = length // 3
         row = iota((length, length), 0)
         column = iota((length, length), 1)
@@ -82,7 +82,7 @@
 def scale_rows(ref, q, j, width):
     r = iota((32, width), 0)
     block = (3 * r + j) // 32
-    rows = [ref[3 * q + n] if len(ref.shape) == 3 else ref[pl.ds(3 * q + n, 1), :] for n in range(3)]
+    rows = [ref[3 * q + n] for n in range(3)]
     return jnp.where(block == 0, rows[0], jnp.where(block == 1, rows[1], rows[2]))
 
 
@@ -93,24 +93,24 @@
         out[pl.ds(pl.multiple_of(base + third * j, 32), 32), :] = values.astype(BF16)
 
 
-def dequant_wide(codes, scales, out, first, last):
-    def step(q, carry):
-        dequant_in(codes, scales, out, q, (q // 4) * 384 + (q % 4) * 32, 128)
+def dequant_wide(codes, scales, out, half):
+    def step(n, carry):
+        dequant_in(codes, scales, out, 15 * half + n, HALF * half + (n // 4) * 384 + (n % 4) * 32, 128)
         return carry
 
-    lax.fori_loop(first, min(last, 28), step, 0)
-    for q in range(28, last):
-        dequant_in(codes, scales, out, q, 2688 + (q - 28) * 32, 64)
+    lax.fori_loop(0, 12, step, 0)
+    for n in range(3):
+        dequant_in(codes, scales, out, 15 * half + 12 + n, HALF * half + 1152 + 32 * n, 96)
 
 
 def layer_kernel(
     tokens_ref, routes_ref, router_ref, drafter_ref, gain, gc, gs, uc, us, dc, ds, normed_ref, wall,
-    tokv, routev, routerv, agb, snd, xr, ret, wide_codes, wide_scales, dcv, dsv, wg, wu, wd, comb, wz, hid,
+    tokv, routev, routerv, agb, snd, xr, back_rows, ret, wide_codes, wide_scales, dcv, dsv, dsh, wg, wu, wd, comb, metas, slab, hid,
     maj, mnr, sall, in_sem, code_sem, zsend, zrecv, psend, precv, loc, qsend, qrecv, qloc,
     rsend, rrecv, xsend, xrecv, wsend, wrecv, wloc,
 ):
     group, wide, y, z, x, c = place()
-    p_me = y * 8 + x * 2 + c
+    me = group * PLANE + y * 8 + x * 2 + c
     sigma = 1 - 2 * c
     y4 = 2 * group + y
 
@@ -138,30 +138,25 @@
         copy.start()
 
     barrier = pltpu.get_barrier_semaphore()
-    for neighbour in (left, right, along_y(1), along_y(3)):
+    for neighbour in (left, right):
         pl.semaphore_signal(barrier, inc=1, device_id=neighbour, device_id_type=MESH)
 
+    def plane_device(n):
+        return (n // PLANE, plane_wide(n % PLANE, z))
+
     def greet(j, carry):
-        p = (p_me + j) % PLANE
-        pl.semaphore_signal(barrier, inc=1, device_id=(group, plane_wide(p, z)), device_id_type=MESH)
+        pl.semaphore_signal(barrier, inc=1, device_id=plane_device((me + j) % ALL), device_id_type=MESH)
         return carry
 
-    lax.fori_loop(1, PLANE, greet, 0)
-
-    def greet_other(j, carry):
-        p = (1 - y) * 8 + j
-        pl.semaphore_signal(barrier, inc=1, device_id=(1 - group, plane_wide(p, z)), device_id_type=MESH)
-        return carry
-
-    lax.fori_loop(0, 8, greet_other, 0)
+    lax.fori_loop(1, ALL, greet, 0)
 
     for copy in loads:
         copy.wait()
     columns = tokv[...]
     column = 0
-    for part in spread(columns):
+    for part in spread(tokv[pl.ds(pl.multiple_of(HALF * group, 16), HALF), :]):
         width = part.shape[1]
-        agb[z, 0:SLABS, :, column : column + width] = part.astype(F32).reshape(SLABS, SLOT, width).astype(BF16)
+        agb[z, :, :, column : column + width] = part.astype(F32).reshape(SLABS, SLOT, width).astype(BF16)
         column += width
     weight = jax.nn.sigmoid(dot_first(routerv[...], columns))
     named_expert = iota((TOK, TOK), 0)
@@ -173,45 +168,48 @@
         routes.append(route.astype(F32))
         high.append(top)
         low.append(chosen - top)
-    line = jnp.concatenate(routes + high + low + [jnp.zeros((1, D - 12 * TOK), F32)], axis=1)
-    drafter = jnp.concatenate([drafter_ref[...].astype(F32), line, jnp.zeros((1, D), F32)], axis=0)
-    agb[z, SLABS] = drafter.astype(BF16)
-    pl.semaphore_wait(barrier, 27)
+    line = jnp.concatenate(routes + high + low, axis=1)
+    metas[z] = jnp.broadcast_to(line, (SLOT, 12 * TOK)).astype(BF16)
+    slab[...] = jnp.concatenate([drafter_ref[...].astype(F32), jnp.zeros((2, D), F32)], axis=0).astype(BF16)
+    pl.semaphore_wait(barrier, 33)
 
     sends = []
-    halves = (pl.ds(0, 9), pl.ds(9, 8))
-
-    def forward(s, part, device, n):
-        ref = agb.at[s, halves[part]]
+    def pass_z(ref, device, n, part):
         copy = remote(ref, ref, zsend.at[n, part], zrecv.at[n, part], device)
         copy.start()
         sends.append(copy)
 
-    def arrived(s, part, n):
-        ref = agb.at[s, halves[part]]
+    def forward(s, device, n):
+        pass_z(metas.at[s], device, n, 0)
+        pass_z(agb.at[s], device, n, 1)
+
+    def got_z(ref, n, part):
         remote(ref, ref, zsend.at[n, part], zrecv.at[n, part], right).wait_recv()
+
+    def arrived(s, n):
+        got_z(metas.at[s], n, 0)
+        got_z(agb.at[s], n, 1)
 
     upper = (iota((TOK, TOK), 0) < iota((TOK, TOK), 1)).astype(F32).astype(BF16)
     p_rows = iota((PLANE, 1), 0)
     experts = ((p_rows // 8) * 64 + z * 8 + p_rows % 8).astype(F32)
 
-    def plane_send(target, s, send_sem, recv_sem):
+    def plane_send(start, source, target, s, send_sem, recv_sem):
         def send(j, carry):
-            p = (p_me + j) % PLANE
-            across = ((p // 8 + y) % 2) * (s % 2)
+            n = (me + j) % ALL
             remote(
-                snd.at[s, p], target.at[s, p_me], send_sem.at[s], recv_sem.at[s],
-                ((group + across) % 2, plane_wide(p, z)),
+                source.at[s, n % start], target.at[s, me], send_sem.at[s], recv_sem.at[s], plane_device(n)
             ).start()
             return carry
 
-        lax.fori_loop(1, PLANE, send, 0)
+        lax.fori_loop(1, ALL, send, 0)
 
     def plane_copies(target, s, send_sem, recv_sem):
-        return remote(snd.at[s, pl.ds(0, 15)], target.at[s, pl.ds(0, 15)], send_sem.at[s], recv_sem.at[s], core)
+        ref = target.at[s, pl.ds(0, ALL - 1)]
+        return remote(ref, ref, send_sem.at[s], recv_sem.at[s], core)
 
     def relay(s):
-        meta = agb[s, SLABS, :, 0 : 12 * TOK].astype(F32)[META : META + 1, :]
+        meta = metas[s].astype(F32)[0:1, :]
         named = jnp.zeros((PLANE, TOK), F32)
         weight = jnp.zeros((PLANE, TOK), F32)
         for k in range(4):
@@ -222,15 +220,15 @@
         rank = dot(named.astype(BF16), upper)
         slot = iota((PLANE, SLOT, TOK), 1, F32)
         pick = jnp.where(rank[:, None, :] == slot, named[:, None, :], 0.0)
-        rows = dot(pick.reshape(TOK, TOK).astype(BF16), agb[s, 0:SLABS].reshape(TOK, D))
-        snd[s] = rows.reshape(PLANE, SLOT, D).astype(BF16)
-        pltpu.make_async_copy(snd.at[s, p_me], xr.at[s, p_me], loc.at[s]).start()
-        plane_send(xr, s, psend, precv)
+        rows = dot(pick.reshape(TOK, TOK).astype(BF16), agb[s].reshape(TOK, HALF))
+        snd[s] = rows.reshape(PLANE, SLOT, HALF).astype(BF16)
+        pltpu.make_async_copy(snd.at[s, me % PLANE], xr.at[s, me], loc.at[s]).start()
+        plane_send(PLANE, snd, xr, s, psend, precv)
         weighted = (pick * weight[:, None, :]).reshape(TOK, TOK).T
+        weighted = jnp.concatenate([weighted, weighted], axis=1)
         top = weighted.astype(BF16)
         comb[s, 0] = top
         comb[s, 1] = (weighted - top.astype(F32)).astype(BF16)
-        wz[s] = agb[s, SLABS]
 
     def source(d):
         return (z + 8 + d * sigma) % 8
@@ -239,154 +237,169 @@
     order_column = iota((UNITS, UNITS), 1)
 
     def experts_on(*distances):
-        inputs = []
+        lower, upper_half = [], []
         for d in distances:
             s = source(d)
-            pltpu.make_async_copy(snd.at[s, p_me], xr.at[s, p_me], loc.at[s]).wait()
+            pltpu.make_async_copy(snd.at[s, 0], xr.at[s, 0], loc.at[s]).wait()
             plane_copies(xr, s, psend, precv).wait_recv()
-            inputs.append(xr[s].reshape(TOK, D))
-        inputs = jnp.concatenate(inputs, axis=0)
-        act = (jax.nn.silu(dot(inputs, wg[...])) * dot(inputs, wu[...])).astype(BF16)
+            lower.append(xr[s, 0:PLANE].reshape(TOK, HALF))
+            upper_half.append(xr[s, PLANE:ALL].reshape(TOK, HALF))
+        lower = jnp.concatenate(lower, axis=0)
+        upper_half = jnp.concatenate(upper_half, axis=0)
+        gate = dot(lower, wg[0:HALF]) + dot(upper_half, wg[HALF:D])
+        act = (jax.nn.silu(gate) * (dot(lower, wu[0:HALF]) + dot(upper_half, wu[HALF:D]))).astype(BF16)
         order = (order_row == 3 * (order_column % 256) + order_column // 256).astype(F32).astype(BF16)
         act = dot(act, order).astype(BF16)
         for n, d in enumerate(distances):
             hid[pl.ds(pl.multiple_of(TOK * source(d), TOK), TOK), :] = act[n * TOK : (n + 1) * TOK]
 
-    def dequant_down(first, last):
-        def step(q, carry):
-            words = dcv[pl.ds(pl.multiple_of(32 * q, 32), 32), :]
-            for j in range(3):
-                values = unpack(words, j, scale_rows(dsv, q, j, D))
-                wd[pl.ds(pl.multiple_of(256 * j + 32 * q, 32), 32), :] = values.astype(BF16)
+    def dequant_down(half):
+        def block(start, width):
+            columns = dcv[pl.ds(pl.multiple_of(HALF * half + start, 32), width), :].T
+            lanes = pl.ds(start if width < 128 else pl.multiple_of(start, 128), width)
+            for q in range(8):
+                for j in range(3):
+                    r = iota((32, width), 0)
+                    unit = (3 * r + j) // 32
+                    rows = [dsh[half, 3 * q + n : 3 * q + n + 1, lanes] for n in range(3)]
+                    scales = jnp.where(unit == 0, rows[0], jnp.where(unit == 1, rows[1], rows[2]))
+                    values = unpack(columns[32 * q : 32 * q + 32], j, scales)
+                    wd[half, 256 * j + 32 * q : 256 * j + 32 * q + 32, lanes] = values.astype(BF16)
+
+        def step(n, carry):
+            block(128 * n, 128)
             return carry
 
-        lax.fori_loop(first, last, step, 0)
+        lax.fori_loop(0, 11, step, 0)
+        block(1408, 32)
 
     def beside(n):
         if n == 0:
             gate_codes.wait()
             gate_scales.wait()
-            dequant_wide(wide_codes, wide_scales, wg, 0, 16)
+            dequant_wide(wide_codes, wide_scales, wg, 0)
         elif n == 1:
-            dequant_wide(wide_codes, wide_scales, wg, 16, 30)
+            dequant_wide(wide_codes, wide_scales, wg, 1)
             up_codes.start()
             up_scales.start()
         elif n == 2:
             down_codes.wait()
             down_scales.wait()
-            dequant_down(0, 4)
+            for half in range(2):
+                dsh[half] = dsv[:, HALF * half : HALF * half + HALF]
+            dequant_down(0)
         elif n == 3:
-            dequant_down(4, 8)
-        elif n == 4:
             up_codes.wait()
             up_scales.wait()
-            dequant_wide(wide_codes, wide_scales, wu, 0, 14)
+            dequant_wide(wide_codes, wide_scales, wu, 0)
+        elif n == 4:
+            dequant_wide(wide_codes, wide_scales, wu, 1)
         elif n == 5:
-            dequant_wide(wide_codes, wide_scales, wu, 14, 30)
-
-    for part in range(2):
-        forward(z, part, right, 0)
-        forward(z, part, left, 1)
+            dequant_down(1)
+
+    keep = pltpu.make_async_copy(slab, wall.at[z, x], wloc)
+    keep.start()
+
+    def share_x(j, carry):
+        remote(slab, wall.at[z, x], wsend, wrecv, (group, wide_of(y, z, (x + j) % 4, c))).start()
+        return carry
+
+    lax.fori_loop(1, 4, share_x, 0)
+    three = remote(wall.at[z, pl.ds(0, 3)], wall.at[z, pl.ds(0, 3)], wsend, wrecv, core)
+    forward(z, right, 0)
+    forward(z, left, 1)
     relay(z)
-    beside(0)
+    keep.wait()
+    three.wait()
+    pass_z(wall.at[z], right, 0, 2)
+    pass_z(wall.at[z], left, 1, 2)
     for k in (1, 2, 3):
+        beside(k - 1)
         back, front = (z + 8 - k) % 8, (z + k) % 8
-        far = (z + 8 - 3 * sigma) % 8
-        for part in range(2):
-            arrived(back, part, 2 * k - 2)
-            if k < 3:
-                forward(back, part, right, 2 * k)
-            arrived(front, part, 2 * k - 1)
-            if k < 3:
-                forward(front, part, left, 2 * k + 1)
-            else:
-                forward(far, part, ahead, 6)
-            if part == 0:
-                beside(2 * k - 1)
+        arrived(back, 2 * k - 2)
+        if k < 3:
+            forward(back, right, 2 * k)
+        arrived(front, 2 * k - 1)
+        if k < 3:
+            forward(front, left, 2 * k + 1)
+        else:
+            forward((z + 8 - 3 * sigma) % 8, ahead, 6)
         relay(back)
         relay(front)
-        beside(2 * k)
+        got_z(wall.at[back], 2 * k - 2, 2)
+        if k < 3:
+            pass_z(wall.at[back], right, 2 * k, 2)
+        got_z(wall.at[front], 2 * k - 1, 2)
+        if k < 3:
+            pass_z(wall.at[front], left, 2 * k + 1, 2)
+        else:
+            pass_z(wall.at[(z + 8 - 3 * sigma) % 8], ahead, 6, 2)
+    beside(3)
+    opposite = (z + 4) % 8
+    arrived(opposite, 6)
+    relay(opposite)
+    got_z(wall.at[opposite], 6, 2)
+    beside(4)
     experts_on(0, 1)
-    opposite = (z + 4) % 8
-    arrived(opposite, 0, 6)
-    arrived(opposite, 1, 6)
-    relay(opposite)
+    beside(5)
     experts_on(-1, 2)
     experts_on(-2, 3)
     experts_on(-3)
-    experts_on(4)
 
     def down(d):
         s = source(d)
-        plane_copies(xr, s, psend, precv).wait_send()
-        rows = dot(hid[pl.ds(pl.multiple_of(TOK * s, TOK), TOK), :], wd[...])
-        snd[s] = rows.reshape(PLANE, SLOT, D).astype(BF16)
-        pltpu.make_async_copy(snd.at[s, p_me], ret.at[s, p_me], qloc.at[s]).start()
-        plane_send(ret, s, qsend, qrecv)
+        acts = hid[pl.ds(pl.multiple_of(TOK * s, TOK), TOK), :]
+        for half in range(2):
+            rows = dot(acts, wd[half])
+            back_rows[s, PLANE * half : PLANE * half + PLANE] = rows.reshape(PLANE, SLOT, HALF).astype(BF16)
+        pltpu.make_async_copy(back_rows.at[s, me], ret.at[s, me], qloc.at[s]).start()
+        plane_send(ALL, back_rows, ret, s, qsend, qrecv)
 
     def combined(d):
         s = source(d)
-        pltpu.make_async_copy(snd.at[s, p_me], ret.at[s, p_me], qloc.at[s]).wait()
+        pltpu.make_async_copy(back_rows.at[s, me], ret.at[s, me], qloc.at[s]).wait()
         plane_copies(ret, s, qsend, qrecv).wait_recv()
-        rows = ret[s].reshape(TOK, D)
+        rows = ret[s].reshape(2 * TOK, HALF)
         return dot(comb[s, 0], rows) + dot(comb[s, 1], rows)
 
-    half_rows = (pl.ds(0, 64), pl.ds(64, 64))
-
-    def hop(buffer, k, half, device, n):
-        copy = remote(
-            buffer.at[k, half_rows[half]], buffer.at[k - 1, half_rows[half]],
-            rsend.at[n, k, half], rrecv.at[n, k - 1, half], device,
-        )
+    def hop(buffer, k, device, n):
+        copy = remote(buffer.at[k], buffer.at[k - 1], rsend.at[n, k], rrecv.at[n, k - 1], device)
         copy.start()
         sends.append(copy)
 
-    def landed(buffer, k, half, n):
-        ref = buffer.at[k, half_rows[half]]
-        remote(ref, ref, rsend.at[n, k, half], rrecv.at[n, k, half], ahead).wait_recv()
-
-    def join(buffer, k, half, part, device, n):
-        landed(buffer, k, half, n)
-        rows = half_rows[half]
-        buffer[k, rows] = (buffer[k, rows].astype(F32) + part[64 * half : 64 * half + 64]).astype(BF16)
-        hop(buffer, k, half, device, n)
-
-    down(4)
+    def landed(buffer, k, n):
+        remote(buffer.at[k], buffer.at[k], rsend.at[n, k], rrecv.at[n, k], ahead).wait_recv()
+
+    def join(buffer, k, part, device, n):
+        landed(buffer, k, n)
+        buffer[k] = (buffer[k].astype(F32) + part).astype(BF16)
+        hop(buffer, k, device, n)
+
     down(3)
     down(-3)
+    experts_on(4)
+    down(4)
     maj[4] = combined(4).astype(BF16)
-    hop(maj, 4, 0, ahead, 0)
-    hop(maj, 4, 1, ahead, 0)
+    hop(maj, 4, ahead, 0)
     down(2)
     down(-2)
-    mnr[3] = combined(-3).astype(BF16)
-    hop(mnr, 3, 0, behind, 1)
-    hop(mnr, 3, 1, behind, 1)
-    part = combined(3)
-    join(maj, 3, 0, part, ahead, 0)
-    join(maj, 3, 1, part, ahead, 0)
+    part, minor = combined(3), combined(-3)
+    mnr[3] = minor.astype(BF16)
+    hop(mnr, 3, behind, 1)
+    join(maj, 3, part, ahead, 0)
     down(1)
     down(-1)
     part, minor = combined(2), combined(-2)
-    for half in range(2):
-        join(mnr, 2, half, minor, behind, 1)
-        join(maj, 2, half, part, ahead, 0)
+    join(mnr, 2, minor, behind, 1)
+    join(maj, 2, part, ahead, 0)
     down(0)
 
-    keep = pltpu.make_async_copy(wz, wall.at[x], wloc)
-    keep.start()
-
-    def share_x(j, carry):
-        remote(wz, wall.at[x], wsend, wrecv, (group, wide_of(y, z, (x + j) % 4, c))).start()
-        return carry
-
-    lax.fori_loop(1, 4, share_x, 0)
-
     part, minor = combined(1), combined(-1)
-    for half in range(2):
-        join(mnr, 1, half, minor, behind, 1)
-        join(maj, 1, half, part, ahead, 0)
+    join(mnr, 1, minor, behind, 1)
+    join(maj, 1, part, ahead, 0)
     part = combined(0)
+
+    half_rows = (pl.ds(0, 64), pl.ds(64, 64))
 
     def pass_y(owner, half, step, n):
         ref = sall.at[owner, half_rows[half]]
@@ -399,11 +412,10 @@
         remote(ref, ref, xsend.at[n, half], xrecv.at[n, half], core).wait_recv()
 
     below, above, across_y = (y4 + 3) % 4, (y4 + 1) % 4, (y4 + 2) % 4
-    for half, rows in enumerate(half_rows):
-        landed(mnr, 0, half, 1)
-        landed(maj, 0, half, 0)
-        total = part[64 * half : 64 * half + 64] + mnr[0, rows].astype(F32) + maj[0, rows].astype(F32)
-        sall[y4, rows] = total.astype(BF16)
+    landed(mnr, 0, 1)
+    landed(maj, 0, 0)
+    sall[y4] = (part + mnr[0].astype(F32) + maj[0].astype(F32)).astype(BF16)
+    for half in range(2):
         pass_y(y4, half, 1, 0)
         pass_y(y4, half, 3, 1)
     got_y(below, 0, 0)
@@ -415,16 +427,14 @@
     for half, rows in enumerate(half_rows):
         got_y(across_y, half, 2)
         for q in range(2):
-            feature = (sall[q, rows].astype(F32) + sall[q + 2, rows].astype(F32)).astype(BF16).astype(F32)
+            feature = jnp.concatenate([sall[q, rows].astype(F32), sall[q + 2, rows].astype(F32)], axis=1)
             mean_square = jnp.sum(feature * feature, axis=1, keepdims=True) / D
-            normed_ref[q, rows] = (feature * lax.rsqrt(mean_square + 1e-05) * gain[...]).astype(BF16)
+            normed_ref[q, rows] = (feature * lax.rsqrt(mean_square + 1e-05) * gain[...].reshape(1, D)).astype(BF16)
     for copy in sends:
         copy.wait_send()
     for s in range(NZ):
+        plane_copies(xr, s, psend, precv).wait_send()
         plane_copies(ret, s, qsend, qrecv).wait_send()
-    keep.wait()
-    three = remote(wall.at[pl.ds(0, 3)], wall.at[pl.ds(0, 3)], wsend, wrecv, core)
-    three.wait()
 
 
 def drafter_kernel(
@@ -469,7 +479,7 @@
     follow.wait()
 
     feature, column = iota((UNITS, 256), 0), iota((UNITS, 256), 1)
-    x_of, z_of, i_of = column // 64, (column // 8) % 8, column % 8
+    x_of, z_of, i_of = (column // 8) % 4, column // 32, column % 8
     choose = ((feature == y * 384 + z_of * 48 + x_of * 12 + c * 6 + i_of) & (i_of < 6)).astype(F32).astype(BF16)
     row = iota((TOK, 1), 0)
     last_chip = chip == 31
@@ -499,7 +509,7 @@
     lax.fori_loop(1, 4, send_err, 0)
 
     before_order, after_order = iota((256, 192), 0), iota((256, 192), 1)
-    matched = before_order == (after_order // 6 % 4) * 64 + (after_order // 24) * 8 + after_order % 6
+    matched = before_order == (after_order // 6 % 4) * 8 + (after_order // 24) * 32 + after_order % 6
     compact = matched.astype(F32).astype(BF16)
     factors = []
     for core_of in range(2):
@@ -531,7 +541,7 @@
     others = remote(err.at[pl.ds(0, 3)], eall.at[pl.ds(0, 3)], esem.at[0], esem.at[1], core)
     others.wait()
     mixed, where_to = iota((1024, UNITS), 0), iota((1024, UNITS), 1)
-    i_of, z_of, x_of, n_of = mixed % 8, (mixed // 8) % 8, (mixed // 64) % 4, mixed // 256
+    i_of, x_of, z_of, n_of = mixed % 8, (mixed // 8) % 4, (mixed // 32) % 8, mixed // 256
     matched = where_to == (n_of // 2) * 384 + z_of * 48 + x_of * 12 + (n_of % 2) * 6 + i_of
     restore = (matched & (i_of < 6)).astype(F32).astype(BF16)
     every = jnp.concatenate([eall[n] for n in range(4)], axis=1)
@@ -589,42 +599,47 @@
     drafter_weight,
 ):
     dma = pltpu.SemaphoreType.DMA
-    frame = (NZ, PLANE, SLOT, D)
+    frame = (NZ, PLANE, SLOT, HALF)
+    double = (NZ, ALL, SLOT, HALF)
     normed, wall = pl.pallas_call(
         layer_kernel,
-        out_shape=(out((2, TOK, D)), out((4, NZ, SLOT, D))),
+        out_shape=(out((2, TOK, D)), out((NZ, 4, SLOT, D))),
         in_specs=[ANY] * 3 + [VM] * 2 + [ANY] * 6,
         out_specs=(VM, ANY),
         scratch_shapes=[
             pltpu.VMEM((D, TOK), BF16),
             pltpu.VMEM((4, TOK), jnp.int32),
             pltpu.VMEM((D, TOK), BF16),
-            pltpu.VMEM((NZ, BLOCKS, SLOT, D), BF16),
             pltpu.VMEM(frame, BF16),
             pltpu.VMEM(frame, BF16),
-            pltpu.VMEM(frame, BF16),
+            pltpu.VMEM(double, BF16),
+            pltpu.VMEM(double, BF16),
+            pltpu.VMEM(double, BF16),
             pltpu.VMEM((WORDS, UNITS), jnp.int32),
             pltpu.VMEM((90, 1, UNITS), jnp.int32),
-            pltpu.VMEM((256, D), jnp.int32),
+            pltpu.VMEM((D, 256), jnp.int32),
             pltpu.VMEM((24, D), jnp.int32),
+            pltpu.VMEM((2, 24, HALF), jnp.int32),
             pltpu.VMEM((D, UNITS), BF16),
             pltpu.VMEM((D, UNITS), BF16),
-            pltpu.VMEM((UNITS, D), BF16),
-            pltpu.VMEM((NZ, 2, TOK, TOK), BF16),
-            pltpu.VMEM((NZ, SLOT, D), BF16),
+            pltpu.VMEM((2, UNITS, HALF), BF16),
+            pltpu.VMEM((NZ, 2, TOK, 2 * TOK), BF16),
+            pltpu.VMEM((NZ, SLOT, 12 * TOK), BF16),
+            pltpu.VMEM((SLOT, D), BF16),
             pltpu.VMEM((1024, UNITS), BF16),
-            pltpu.VMEM((5, TOK, D), BF16),
-            pltpu.VMEM((4, TOK, D), BF16),
-            pltpu.VMEM((4, TOK, D), BF16),
-            dma((3,)), dma((6,)), dma((7, 2)), dma((7, 2)), dma((NZ,)), dma((NZ,)), dma((NZ,)),
-            dma((NZ,)), dma((NZ,)), dma((NZ,)), dma((2, 5, 2)), dma((2, 5, 2)), dma((3, 2)), dma((3, 2)),
+            pltpu.VMEM((5, TOK, HALF), BF16),
+            pltpu.VMEM((4, TOK, HALF), BF16),
+            pltpu.VMEM((4, TOK, HALF), BF16),
+            dma((3,)), dma((6,)), dma((7, 3)), dma((7, 3)), dma((NZ,)), dma((NZ,)), dma((NZ,)),
+            dma((NZ,)), dma((NZ,)), dma((NZ,)), dma((2, 5)), dma((2, 5)), dma((3, 2)), dma((3, 2)),
             dma, dma, dma,
         ],
         compiler_params=params(1),
         name="layer",
     )(
-        tokens.T, routes.T, router, drafter_weight, norm_gain[None, :], gate_codes[0],
-        gate_scales.transpose(1, 0, 2), up_codes[0], up_scales.transpose(1, 0, 2), down_codes[0], down_scales[0],
+        tokens.T, routes.T, router, drafter_weight, norm_gain, gate_codes[0],
+        gate_scales.transpose(1, 0, 2), up_codes[0], up_scales.transpose(1, 0, 2),
+        down_codes[0].T, down_scales[0],
     )
     grad_scale = 1.0 / math.sqrt(TOK * lax.axis_size("wide"))
     error, gradient = pl.pallas_call(

time: 249 us -> 235 us (0.944)
  Pallas kernels: 240 us -> 229 us
  local copies, waits for them, and re-layouts: 7.81 us -> 3.03 us
    pallas_call x1, Pallas kernels: 199 us -> 183 us  [shards(): pl.pallas_call(layer_kernel, out_shape=(out((2, TOK, D)), out((NZ, 4, SLO...]
    pallas_call x1, Pallas kernels: 41.4 us -> 46.3 us  [shards(): pl.pallas_call(functools.partial(drafter_kernel, grad_scale), out_shape=(...]
    unnamed x3 -> x2, local copies, waits for them, and re-layouts: 6.5 us -> 3.03 us
where the time goes in v3:
time: 235 us; the launch traced here: 233 us
  Pallas kernels  229 us (97%)
  local copies, waits for them, and re-layouts  3.03 us (1%)
    pallas_call x1, Pallas kernels, shards(): pl.pallas_call(layer_kernel, out_shape=(out((2, TOK, D)), out((NZ, 4, SLO...  183 us
    pallas_call x1, Pallas kernels, shards(): pl.pallas_call(functools.partial(drafter_kernel, grad_scale), out_shape=(...  46.3 us

profile of v3, /device:TPU:16, one launch (start us, length us, event | category | flops | bytes accessed | tf_op | source)
XLA Modules:
  0.0 232.5 jit_solution(5021442499463164767)
XLA Ops:
  0.6 182.6 %layer.1 = (bf16[2,128,2880]{2,1,0:T(8,128)(2,1)}, bf16[8,4,8,2880]{3,2,1,0:T(8,128)(2,1)}) custom-call(bf16[2880,128]{1,0:T(8,128)(2,1)} %bitcast.14, s32[4,128]{1,0:T(4,128)} %bitcast.19, bf16[2880,128]{1,0:T(8,128)(2,1)} %router_ref.1, bf16[6,2880]{1,0:T(8,128)(2,1)} %drafter_ref.1, f32[2880]{0:T(1024)} %gain.1, s32[960,768]{1,0:T(8,128)} %bitcast.11, ...), custom_call_target="tpu_custom_call" | custom-call | tf_op jit(solution)/shard_map/layer/pallas_call | solution.py:604
  183.2 46.3 %drafter.1 = (bf16[128,768]{1,0:T(8,128)(2,1)}, bf16[8,2880]{1,0:T(8,128)(2,1)}) custom-call(bf16[2,128,2880]{2,1,0:T(8,128)(2,1)} %get-tuple-element.6.normed, bf16[8,4,8,2880]{3,2,1,0:T(8,128)(2,1)} %get-tuple-element.7.wall), custom_call_target="tpu_custom_call" | custom-call | tf_op jit(solution)/shard_map/drafter/pallas_call | solution.py:645
  229.5 1.6 copy.15
  231.1 1.4 copy.16

commit v4 on v3

--- a/solution.py
+++ b/solution.py
@@ -104,10 +104,11 @@
 
 
 def layer_kernel(
-    tokens_ref, routes_ref, router_ref, drafter_ref, gain, gc, gs, uc, us, dc, ds, normed_ref, wall,
-    tokv, routev, routerv, agb, snd, xr, back_rows, ret, wide_codes, wide_scales, dcv, dsv, dsh, wg, wu, wd, comb, metas, slab, hid,
+    grad_scale, tokens_ref, routes_ref, router_ref, drafter_ref, gain, gc, gs, uc, us, dc, ds, error_ref, grad_ref,
+    tokv, routev, routerv, agb, snd, xr, ret, wide_codes, wide_scales, dcv, dsv, dsh, wg, wu, wd, comb, metas, slab, hid,
     maj, mnr, sall, in_sem, code_sem, zsend, zrecv, psend, precv, loc, qsend, qrecv, qloc,
-    rsend, rrecv, xsend, xrecv, wsend, wrecv, wloc,
+    rsend, rrecv, lsend, lrecv, xsend, xrecv, wsend, wrecv, wloc,
+    wall, nall, first, err, eall, gsum, gmaj, gmnr, pieces, fin, fsem, nsend, nrecv, esem, gsend, grecv, fsend, frecv, dloc,
 ):
     group, wide, y, z, x, c = place()
     me = group * PLANE + y * 8 + x * 2 + c
@@ -138,7 +139,11 @@
         copy.start()
 
     barrier = pltpu.get_barrier_semaphore()
-    for neighbour in (left, right):
+    chip = z * 4 + x
+    before, after = (chip + 31) % 32, (chip + 1) % 32
+    before = (group, wide_of(y, before // 4, before % 4, c))
+    after = (group, wide_of(y, after // 4, after % 4, c))
+    for neighbour in (left, right, before, after):
         pl.semaphore_signal(barrier, inc=1, device_id=neighbour, device_id_type=MESH)
 
     def plane_device(n):
@@ -171,7 +176,7 @@
     line = jnp.concatenate(routes + high + low, axis=1)
     metas[z] = jnp.broadcast_to(line, (SLOT, 12 * TOK)).astype(BF16)
     slab[...] = jnp.concatenate([drafter_ref[...].astype(F32), jnp.zeros((2, D), F32)], axis=0).astype(BF16)
-    pl.semaphore_wait(barrier, 33)
+    pl.semaphore_wait(barrier, 35)
 
     sends = []
     def pass_z(ref, device, n, part):
@@ -221,7 +226,7 @@
         slot = iota((PLANE, SLOT, TOK), 1, F32)
         pick = jnp.where(rank[:, None, :] == slot, named[:, None, :], 0.0)
         rows = dot(pick.reshape(TOK, TOK).astype(BF16), agb[s].reshape(TOK, HALF))
-        snd[s] = rows.reshape(PLANE, SLOT, HALF).astype(BF16)
+        snd[s, 0:PLANE] = rows.reshape(PLANE, SLOT, HALF).astype(BF16)
         pltpu.make_async_copy(snd.at[s, me % PLANE], xr.at[s, me], loc.at[s]).start()
         plane_send(PLANE, snd, xr, s, psend, precv)
         weighted = (pick * weight[:, None, :]).reshape(TOK, TOK).T
@@ -348,16 +353,17 @@
 
     def down(d):
         s = source(d)
+        plane_copies(xr, s, psend, precv).wait_send()
         acts = hid[pl.ds(pl.multiple_of(TOK * s, TOK), TOK), :]
         for half in range(2):
             rows = dot(acts, wd[half])
-            back_rows[s, PLANE * half : PLANE * half + PLANE] = rows.reshape(PLANE, SLOT, HALF).astype(BF16)
-        pltpu.make_async_copy(back_rows.at[s, me], ret.at[s, me], qloc.at[s]).start()
-        plane_send(ALL, back_rows, ret, s, qsend, qrecv)
+            snd[s, PLANE * half : PLANE * half + PLANE] = rows.reshape(PLANE, SLOT, HALF).astype(BF16)
+        pltpu.make_async_copy(snd.at[s, me], ret.at[s, me], qloc.at[s]).start()
+        plane_send(ALL, snd, ret, s, qsend, qrecv)
 
     def combined(d):
         s = source(d)
-        pltpu.make_async_copy(back_rows.at[s, me], ret.at[s, me], qloc.at[s]).wait()
+        pltpu.make_async_copy(snd.at[s, me], ret.at[s, me], qloc.at[s]).wait()
         plane_copies(ret, s, qsend, qrecv).wait_recv()
         rows = ret[s].reshape(2 * TOK, HALF)
         return dot(comb[s, 0], rows) + dot(comb[s, 1], rows)
@@ -395,11 +401,22 @@
     down(0)
 
     part, minor = combined(1), combined(-1)
-    join(mnr, 1, minor, behind, 1)
-    join(maj, 1, part, ahead, 0)
+    half_rows = (pl.ds(0, 64), pl.ds(64, 64))
+
+    def last(buffer, half, device, n):
+        copy = remote(
+            buffer.at[1, half_rows[half]], buffer.at[0, half_rows[half]], lsend.at[n, half], lrecv.at[n, half], device
+        )
+        copy.start()
+        sends.append(copy)
+
+    landed(mnr, 1, 1)
+    landed(maj, 1, 0)
+    for half, rows in enumerate(half_rows):
+        for n, (buffer, more, device) in enumerate(((maj, part, ahead), (mnr, minor, behind))):
+            buffer[1, rows] = (buffer[1, rows].astype(F32) + more[64 * half : 64 * half + 64]).astype(BF16)
+            last(buffer, half, device, n)
     part = combined(0)
-
-    half_rows = (pl.ds(0, 64), pl.ds(64, 64))
 
     def pass_y(owner, half, step, n):
         ref = sall.at[owner, half_rows[half]]
@@ -412,10 +429,13 @@
         remote(ref, ref, xsend.at[n, half], xrecv.at[n, half], core).wait_recv()
 
     below, above, across_y = (y4 + 3) % 4, (y4 + 1) % 4, (y4 + 2) % 4
-    landed(mnr, 0, 1)
-    landed(maj, 0, 0)
-    sall[y4] = (part + mnr[0].astype(F32) + maj[0].astype(F32)).astype(BF16)
-    for half in range(2):
+    for half, rows in enumerate(half_rows):
+        total = part[64 * half : 64 * half + 64]
+        for n, buffer in enumerate((maj, mnr)):
+            ref = buffer.at[0, rows]
+            remote(ref, ref, lsend.at[n, half], lrecv.at[n, half], ahead).wait_recv()
+            total = total + buffer[0, rows].astype(F32)
+        sall[y4, rows] = total.astype(BF16)
         pass_y(y4, half, 1, 0)
         pass_y(y4, half, 3, 1)
     got_y(below, 0, 0)
@@ -424,53 +444,20 @@
     pass_y(above, 1, 3, 2)
     got_y(below, 1, 0)
     got_y(above, 0, 1)
+    swaps = []
     for half, rows in enumerate(half_rows):
         got_y(across_y, half, 2)
         for q in range(2):
             feature = jnp.concatenate([sall[q, rows].astype(F32), sall[q + 2, rows].astype(F32)], axis=1)
             mean_square = jnp.sum(feature * feature, axis=1, keepdims=True) / D
-            normed_ref[q, rows] = (feature * lax.rsqrt(mean_square + 1e-05) * gain[...].reshape(1, D)).astype(BF16)
-    for copy in sends:
-        copy.wait_send()
-    for s in range(NZ):
-        plane_copies(xr, s, psend, precv).wait_send()
-        plane_copies(ret, s, qsend, qrecv).wait_send()
-
-
-def drafter_kernel(
-    grad_scale, normed, wall, error_ref, grad_ref,
-    nall, first, err, eall, gsum, maj, mnr, slab, fin, fsem, nsem, esem, rsend, rrecv, psend, precv, loc,
-):
-    group, wide, y, z, x, c = place()
-    core = (group, wide_of(y, z, x, 1 - c))
-    chip = z * 4 + x
-    before, after = (chip + 31) % 32, (chip + 1) % 32
-    before = (group, wide_of(y, before // 4, before % 4, c))
-    after = (group, wide_of(y, after // 4, after % 4, c))
-    sigma = 1 - 2 * c
-    ahead = (group, wide_of(y, (z + 8 + sigma) % 8, x, c))
-    behind = (group, wide_of(y, (z + 8 - sigma) % 8, x, c))
-    me = y * 2 + c
-
-    def mate(j):
-        n = (me + j) % 4
-        return (group, wide_of(n // 2, z, x, n % 2))
-
-    def peer(j):
-        return (group, wide_of(y, z, (x + j) % 4, c))
-
-    barrier = pltpu.get_barrier_semaphore()
-    for neighbour in (ahead, behind, before, after, mate(1), mate(2), mate(3), peer(1), peer(2), peer(3)):
-        pl.semaphore_signal(barrier, inc=1, device_id=neighbour, device_id_type=MESH)
-    pl.semaphore_wait(barrier, 10)
-
-    keep = pltpu.make_async_copy(normed, nall.at[c], loc.at[0])
-    keep.start()
-    swap = remote(normed, nall.at[c], nsem.at[0], nsem.at[1], core)
-    swap.start()
+            nall[c, q, rows] = (feature * lax.rsqrt(mean_square + 1e-05) * gain[...].reshape(1, D)).astype(BF16)
+        ref = nall.at[c, :, rows]
+        swap = remote(ref, ref, nsend.at[half], nrecv.at[half], core)
+        swap.start()
+        swaps.append(swap)
     lanes = pl.ds(pl.multiple_of(group * UNITS, 128), UNITS)
-    keep.wait()
-    swap.wait()
+    for swap in swaps:
+        swap.wait()
     follow = remote(nall.at[0, :, pl.ds(0, 16), lanes], first, fsem.at[0], fsem.at[1], before)
     follow.start()
     predicted = lax.dot_general(
@@ -483,6 +470,7 @@
     choose = ((feature == y * 384 + z_of * 48 + x_of * 12 + c * 6 + i_of) & (i_of < 6)).astype(F32).astype(BF16)
     row = iota((TOK, 1), 0)
     last_chip = chip == 31
+    quad = y * 2 + c
     for core_of in range(2):
         for y_of in range(2):
             own = nall[core_of, y_of, :, lanes].astype(F32)
@@ -496,13 +484,13 @@
             position = wide_of(y_of, z, x, core_of) * TOK + row
             residual = jnp.where(position < 128 * TOK - 1, residual, 0.0).astype(BF16)
             err[y_of * 2 + core_of] = residual
-    keep_err = pltpu.make_async_copy(err.at[me], eall.at[me], loc.at[1])
+    keep_err = pltpu.make_async_copy(err.at[quad], eall.at[quad], dloc.at[0])
     keep_err.start()
 
     def send_err(j, carry):
-        n = (me + j) % 4
+        n = (quad + j) % 4
         remote(
-            err.at[n], eall.at[me], esem.at[0], esem.at[1], (group, wide_of(n // 2, z, x, n % 2))
+            err.at[n], eall.at[quad], esem.at[0], esem.at[1], (group, wide_of(n // 2, z, x, n % 2))
         ).start()
         return carry
 
@@ -522,20 +510,18 @@
         s = (z + 8 + d * sigma) % 8
         return gsum[pl.ds(pl.multiple_of(24 * s, 8), 24), :].reshape(3, SLOT, D)
 
-    sends = []
-
-    def hop(buffer, k, device, n):
-        copy = remote(buffer.at[k], buffer.at[k - 1], rsend.at[n, k], rrecv.at[n, k - 1], device)
+    def ghop(buffer, k, device, n):
+        copy = remote(buffer.at[k], buffer.at[k - 1], gsend.at[n, k], grecv.at[n, k - 1], device)
         copy.start()
         sends.append(copy)
 
-    def landed(buffer, k, n):
-        remote(buffer.at[k], buffer.at[k], rsend.at[n, k], rrecv.at[n, k], ahead).wait_recv()
-
-    maj[4] = own_part(4).astype(BF16)
-    hop(maj, 4, ahead, 0)
-    mnr[3] = own_part(-3).astype(BF16)
-    hop(mnr, 3, behind, 1)
+    def glanded(buffer, k, n):
+        remote(buffer.at[k], buffer.at[k], gsend.at[n, k], grecv.at[n, k], ahead).wait_recv()
+
+    gmaj[4] = own_part(4).astype(BF16)
+    ghop(gmaj, 4, ahead, 0)
+    gmnr[3] = own_part(-3).astype(BF16)
+    ghop(gmnr, 3, behind, 1)
 
     keep_err.wait()
     others = remote(err.at[pl.ds(0, 3)], eall.at[pl.ds(0, 3)], esem.at[0], esem.at[1], core)
@@ -548,36 +534,38 @@
     error_ref[...] = dot(every, restore).astype(BF16)
 
     for k in (3, 2, 1):
-        landed(maj, k, 0)
-        maj[k] = (maj[k].astype(F32) + own_part(k)).astype(BF16)
-        hop(maj, k, ahead, 0)
+        glanded(gmaj, k, 0)
+        gmaj[k] = (gmaj[k].astype(F32) + own_part(k)).astype(BF16)
+        ghop(gmaj, k, ahead, 0)
         if k < 3:
-            landed(mnr, k, 1)
-            mnr[k] = (mnr[k].astype(F32) + own_part(-k)).astype(BF16)
-            hop(mnr, k, behind, 1)
-    landed(mnr, 0, 1)
-    landed(maj, 0, 0)
-    total = own_part(0) + mnr[0].astype(F32) + maj[0].astype(F32)
+            glanded(gmnr, k, 1)
+            gmnr[k] = (gmnr[k].astype(F32) + own_part(-k)).astype(BF16)
+            ghop(gmnr, k, behind, 1)
+    glanded(gmnr, 0, 1)
+    glanded(gmaj, 0, 0)
+    total = own_part(0) + gmnr[0].astype(F32) + gmaj[0].astype(F32)
     total = total.reshape(24, D).astype(BF16)
     q, r = iota((32, 24), 0), iota((32, 24), 1)
     expand = ((q // 8) * 6 + q % 8 == r) & (q % 8 < 6)
-    slab[...] = dot(expand.astype(F32).astype(BF16), total).reshape(4, SLOT, D).astype(BF16)
-    keep_fin = pltpu.make_async_copy(slab.at[x], fin.at[x], loc.at[2])
+    pieces[...] = dot(expand.astype(F32).astype(BF16), total).reshape(4, SLOT, D).astype(BF16)
+    keep_fin = pltpu.make_async_copy(pieces.at[x], fin.at[x], dloc.at[1])
     keep_fin.start()
 
     def send(j, carry):
         n = (x + j) % 4
-        remote(slab.at[n], fin.at[x], psend, precv, (group, wide_of(y, z, n, c))).start()
+        remote(pieces.at[n], fin.at[x], fsend, frecv, (group, wide_of(y, z, n, c))).start()
         return carry
 
     lax.fori_loop(1, 4, send, 0)
     keep_fin.wait()
-    whole = remote(slab.at[pl.ds(0, 3)], fin.at[pl.ds(0, 3)], psend, precv, core)
+    whole = remote(pieces.at[pl.ds(0, 3)], fin.at[pl.ds(0, 3)], fsend, frecv, core)
     whole.wait_recv()
     grad_ref[...] = jnp.sum(fin[...].astype(F32), axis=0).astype(BF16)
     whole.wait_send()
     for copy in sends:
         copy.wait_send()
+    for s in range(NZ):
+        plane_copies(ret, s, qsend, qrecv).wait_send()
 
 
 def params(number=None):
@@ -601,16 +589,16 @@
     dma = pltpu.SemaphoreType.DMA
     frame = (NZ, PLANE, SLOT, HALF)
     double = (NZ, ALL, SLOT, HALF)
-    normed, wall = pl.pallas_call(
-        layer_kernel,
-        out_shape=(out((2, TOK, D)), out((NZ, 4, SLOT, D))),
+    grad_scale = 1.0 / math.sqrt(TOK * lax.axis_size("wide"))
+    error, gradient = pl.pallas_call(
+        functools.partial(layer_kernel, grad_scale),
+        out_shape=(out((TOK, UNITS)), out((SLOT, D))),
         in_specs=[ANY] * 3 + [VM] * 2 + [ANY] * 6,
-        out_specs=(VM, ANY),
+        out_specs=(VM, VM),
         scratch_shapes=[
             pltpu.VMEM((D, TOK), BF16),
             pltpu.VMEM((4, TOK), jnp.int32),
             pltpu.VMEM((D, TOK), BF16),
-            pltpu.VMEM(frame, BF16),
             pltpu.VMEM(frame, BF16),
             pltpu.VMEM(double, BF16),
             pltpu.VMEM(double, BF16),
@@ -631,23 +619,9 @@
             pltpu.VMEM((4, TOK, HALF), BF16),
             pltpu.VMEM((4, TOK, HALF), BF16),
             dma((3,)), dma((6,)), dma((7, 3)), dma((7, 3)), dma((NZ,)), dma((NZ,)), dma((NZ,)),
-            dma((NZ,)), dma((NZ,)), dma((NZ,)), dma((2, 5)), dma((2, 5)), dma((3, 2)), dma((3, 2)),
+            dma((NZ,)), dma((NZ,)), dma((NZ,)), dma((2, 5)), dma((2, 5)), dma((2, 2)), dma((2, 2)), dma((3, 2)), dma((3, 2)),
             dma, dma, dma,
-        ],
-        compiler_params=params(1),
-        name="layer",
-    )(
-        tokens.T, routes.T, router, drafter_weight, norm_gain, gate_codes[0],
-        gate_scales.transpose(1, 0, 2), up_codes[0], up_scales.transpose(1, 0, 2),
-        down_codes[0].T, down_scales[0],
-    )
-    grad_scale = 1.0 / math.sqrt(TOK * lax.axis_size("wide"))
-    error, gradient = pl.pallas_call(
-        functools.partial(drafter_kernel, grad_scale),
-        out_shape=(out((TOK, UNITS)), out((SLOT, D))),
-        in_specs=[VM] * 2,
-        out_specs=(VM, VM),
-        scratch_shapes=[
+            pltpu.VMEM((NZ, 4, SLOT, D), BF16),
             pltpu.VMEM((2, 2, TOK, D), BF16),
             pltpu.VMEM((2, 16, UNITS), BF16),
             pltpu.VMEM((4, TOK, 256), BF16),
@@ -657,11 +631,15 @@
             pltpu.VMEM((4, 3, SLOT, D), BF16),
             pltpu.VMEM((4, SLOT, D), BF16),
             pltpu.VMEM((4, SLOT, D), BF16),
-            dma((2,)), dma((2,)), dma((2,)), dma((2, 5)), dma((2, 5)), dma, dma, dma((3,)),
+            dma((2,)), dma((2,)), dma((2,)), dma((2,)), dma((2, 5)), dma((2, 5)), dma, dma, dma((2,)),
         ],
-        compiler_params=params(2),
-        name="drafter",
-    )(normed, wall)
+        compiler_params=params(1),
+        name="layer",
+    )(
+        tokens.T, routes.T, router, drafter_weight, norm_gain, gate_codes[0],
+        gate_scales.transpose(1, 0, 2), up_codes[0], up_scales.transpose(1, 0, 2),
+        down_codes[0].T, down_scales[0],
+    )
     return (error, gradient[:6])
 
 

time: 235 us -> 223 us (0.949)
  Pallas kernels: 229 us -> 216 us
    pallas_call x2 -> x1, Pallas kernels: 229 us -> 216 us  [shards(): pl.pallas_call(functools.partial(layer_kernel, grad_scale), out_shape=(ou...]
where the time goes in v4:
time: 223 us; the launch traced here: 220 us
  Pallas kernels  216 us (97%)
  local copies, waits for them, and re-layouts  3.03 us (1%)
    pallas_call x1, Pallas kernels, shards(): pl.pallas_call(functools.partial(layer_kernel, grad_scale), out_shape=(ou...  216 us

profile of v4, /device:TPU:16, one launch (start us, length us, event | category | flops | bytes accessed | tf_op | source)
XLA Modules:
  0.0 220.1 jit_solution(8010984684990828755)
XLA Ops:
  0.6 216.5 %layer.1 = (bf16[128,768]{1,0:T(8,128)(2,1)}, bf16[8,2880]{1,0:T(8,128)(2,1)}) custom-call(bf16[2880,128]{1,0:T(8,128)(2,1)} %bitcast.14, s32[4,128]{1,0:T(4,128)} %bitcast.19, bf16[2880,128]{1,0:T(8,128)(2,1)} %router_ref.1, bf16[6,2880]{1,0:T(8,128)(2,1)} %drafter_ref.1, f32[2880]{0:T(1024)} %gain.1, s32[960,768]{1,0:T(8,128)} %bitcast.11, ...), custom_call_target="tpu_custom_call" | custom-call | tf_op jit(solution)/shard_map/layer/pallas_call | solution.py:593
  217.1 1.6 copy.15
  218.7 1.4 copy.16

commit v5 on v4

--- a/solution.py
+++ b/solution.py
@@ -385,21 +385,20 @@
     down(-3)
     experts_on(4)
     down(4)
+    down(2)
     maj[4] = combined(4).astype(BF16)
     hop(maj, 4, ahead, 0)
-    down(2)
     down(-2)
     part, minor = combined(3), combined(-3)
     mnr[3] = minor.astype(BF16)
     hop(mnr, 3, behind, 1)
+    down(1)
     join(maj, 3, part, ahead, 0)
-    down(1)
     down(-1)
     part, minor = combined(2), combined(-2)
+    down(0)
     join(mnr, 2, minor, behind, 1)
     join(maj, 2, part, ahead, 0)
-    down(0)
-
     part, minor = combined(1), combined(-1)
     half_rows = (pl.ds(0, 64), pl.ds(64, 64))
 
@@ -456,34 +455,36 @@
         swap.start()
         swaps.append(swap)
     lanes = pl.ds(pl.multiple_of(group * UNITS, 128), UNITS)
+
+    def predict(core_of):
+        return lax.dot_general(
+            nall[core_of].reshape(256, D), wall[...].reshape(256, D), (((1,), (1,)), ((), ())),
+            preferred_element_type=F32,
+        )
+
+    own_part = predict(c)
     for swap in swaps:
         swap.wait()
     follow = remote(nall.at[0, :, pl.ds(0, 16), lanes], first, fsem.at[0], fsem.at[1], before)
     follow.start()
-    predicted = lax.dot_general(
-        nall[...].reshape(512, D), wall[...].reshape(256, D), (((1,), (1,)), ((), ())), preferred_element_type=F32
-    )
-    follow.wait()
-
+    other_part = predict(1 - c)
     feature, column = iota((UNITS, 256), 0), iota((UNITS, 256), 1)
     x_of, z_of, i_of = (column // 8) % 4, column // 32, column % 8
     choose = ((feature == y * 384 + z_of * 48 + x_of * 12 + c * 6 + i_of) & (i_of < 6)).astype(F32).astype(BF16)
+    follow.wait()
     row = iota((TOK, 1), 0)
     last_chip = chip == 31
     quad = y * 2 + c
-    for core_of in range(2):
+    for core_of, predicted in ((c, own_part), (1 - c, other_part)):
         for y_of in range(2):
             own = nall[core_of, y_of, :, lanes].astype(F32)
-            if core_of == 0:
-                following = nall[1, y_of, 0:16, lanes].astype(F32)[0:1, :]
-            else:
-                following = jnp.where(last_chip, first[1 - y_of].astype(F32)[0:1, :], first[y_of].astype(F32)[0:1, :])
+            beside_row = nall[1, y_of, 0:16, lanes].astype(F32)[0:1, :]
+            beyond = jnp.where(last_chip, first[1 - y_of].astype(F32)[0:1, :], first[y_of].astype(F32)[0:1, :])
+            following = jnp.where(core_of == 0, beside_row, beyond)
             target = jnp.where(row == TOK - 1, following, pltpu.roll(own, TOK - 1, 0)).astype(BF16)
-            start = (core_of * 2 + y_of) * TOK
-            residual = predicted[start : start + TOK] - dot(target, choose)
+            residual = predicted[y_of * TOK : y_of * TOK + TOK] - dot(target, choose)
             position = wide_of(y_of, z, x, core_of) * TOK + row
-            residual = jnp.where(position < 128 * TOK - 1, residual, 0.0).astype(BF16)
-            err[y_of * 2 + core_of] = residual
+            err[y_of * 2 + core_of] = jnp.where(position < 128 * TOK - 1, residual, 0.0).astype(BF16)
     keep_err = pltpu.make_async_copy(err.at[quad], eall.at[quad], dloc.at[0])
     keep_err.start()
 

time: 223 us -> 213 us (0.955); the launches traced: 220 us -> 212 us
  Pallas kernels: 216 us -> 209 us
    pallas_call x1, Pallas kernels: 216 us -> 209 us  [shards(): pl.pallas_call(functools.partial(layer_kernel, grad_scale), out_shape=(ou...]
where the time goes in v5:
time: 213 us; the launch traced here: 212 us
  Pallas kernels  209 us (98%)
  local copies, waits for them, and re-layouts  3.03 us (1%)
    pallas_call x1, Pallas kernels, shards(): pl.pallas_call(functools.partial(layer_kernel, grad_scale), out_shape=(ou...  209 us

profile of v5, /device:TPU:16, one launch (start us, length us, event | category | flops | bytes accessed | tf_op | source)
XLA Modules:
  0.0 212.4 jit_solution(10247209735487831120)
XLA Ops:
  0.6 208.8 %layer.1 = (bf16[128,768]{1,0:T(8,128)(2,1)}, bf16[8,2880]{1,0:T(8,128)(2,1)}) custom-call(bf16[2880,128]{1,0:T(8,128)(2,1)} %bitcast.14, s32[4,128]{1,0:T(4,128)} %bitcast.19, bf16[2880,128]{1,0:T(8,128)(2,1)} %router_ref.1, bf16[6,2880]{1,0:T(8,128)(2,1)} %drafter_ref.1, f32[2880]{0:T(1024)} %gain.1, s32[960,768]{1,0:T(8,128)} %bitcast.11, ...), custom_call_target="tpu_custom_call" | custom-call | tf_op jit(solution)/shard_map/layer/pallas_call | solution.py:594
  209.4 1.6 copy.15
  211.0 1.4 copy.16

commit v6 on v5

--- a/solution.py
+++ b/solution.py
@@ -345,12 +345,6 @@
     relay(opposite)
     got_z(wall.at[opposite], 6, 2)
     beside(4)
-    experts_on(0, 1)
-    beside(5)
-    experts_on(-1, 2)
-    experts_on(-2, 3)
-    experts_on(-3)
-
     def down(d):
         s = source(d)
         plane_copies(xr, s, psend, precv).wait_send()
@@ -361,6 +355,13 @@
         pltpu.make_async_copy(snd.at[s, me], ret.at[s, me], qloc.at[s]).start()
         plane_send(ALL, snd, ret, s, qsend, qrecv)
 
+    experts_on(0, 1)
+    beside(5)
+    experts_on(-1, 2)
+    experts_on(-2, 3)
+    down(3)
+    experts_on(-3)
+
     def combined(d):
         s = source(d)
         pltpu.make_async_copy(snd.at[s, me], ret.at[s, me], qloc.at[s]).wait()
@@ -381,10 +382,9 @@
         buffer[k] = (buffer[k].astype(F32) + part).astype(BF16)
         hop(buffer, k, device, n)
 
-    down(3)
-    down(-3)
     experts_on(4)
     down(4)
+    down(-3)
     down(2)
     maj[4] = combined(4).astype(BF16)
     hop(maj, 4, ahead, 0)

time: 213 us -> 211 us (level)
    pallas_call x1, Pallas kernels: 209 us -> 207 us  [shards(): pl.pallas_call(functools.partial(layer_kernel, grad_scale), out_shape=(ou...]
where the time goes in v6:
time: 211 us; the launch traced here: 210 us
  Pallas kernels  207 us (98%)
  local copies, waits for them, and re-layouts  3.03 us (1%)
    pallas_call x1, Pallas kernels, shards(): pl.pallas_call(functools.partial(layer_kernel, grad_scale), out_shape=(ou...  207 us

profile of v6, /device:TPU:16, one launch (start us, length us, event | category | flops | bytes accessed | tf_op | source)
XLA Modules:
  0.0 210.3 jit_solution(3651298410703854710)
XLA Ops:
  0.6 206.6 %layer.1 = (bf16[128,768]{1,0:T(8,128)(2,1)}, bf16[8,2880]{1,0:T(8,128)(2,1)}) custom-call(bf16[2880,128]{1,0:T(8,128)(2,1)} %bitcast.14, s32[4,128]{1,0:T(4,128)} %bitcast.19, bf16[2880,128]{1,0:T(8,128)(2,1)} %router_ref.1, bf16[6,2880]{1,0:T(8,128)(2,1)} %drafter_ref.1, f32[2880]{0:T(1024)} %gain.1, s32[960,768]{1,0:T(8,128)} %bitcast.11, ...), custom_call_target="tpu_custom_call" | custom-call | tf_op jit(solution)/shard_map/layer/pallas_call | solution.py:594
  207.3 1.6 copy.15
  208.9 1.4 copy.16
